TPU v7x, 32 devices: a whole 2x2x4 slice. The times are simulated.
32 devices in a mesh: ctx: 2 (over x), head: 4 (over y, core), exp: 4 (over z).
Axes of the slice: x: 2, y: 2, z: 4, core: 2. Of those that a mesh axis runs over, the one named last changes fastest.
Arguments:
- resid: bfloat16 [1024, 2048], P(('ctx', 'exp')), may hold values from -6 to 6
- queries: bfloat16 [1024, 4096], P(('ctx', 'exp'), 'head'), may hold values from -42 to 42
- rotated_key_value_pairs: bfloat16 [2, 1024, 512], P(None, ('ctx', 'exp'), 'head'), may hold values from -13 to 13
- doc_ids: int32 [1, 1024], P(None, ('ctx', 'exp')), may hold values from 0 to 5, never falling along the last dimension, each value on 1 to 768 neighbouring positions
- out_weight: bfloat16 [4096, 2048], P('head', ('ctx', 'exp')), may hold values from -0.09375 to 0.09375
- norm_gain: float32 [2048], replicated, may hold values from 0.1 to 1.9
- routes: int32 [1024, 8], P(('ctx', 'exp')), may hold values from 0 to 15, all different within a row; in each aligned block of 128 rows (0 to 127, 128 to 255, ...) at most 80 rows name the same one
- probs: float32 [1024, 8], P(('ctx', 'exp')), may hold values from 0.05 to 0.3
- w_gate: bfloat16 [16, 768, 2048], P(('ctx', 'exp'), None, 'head'), may hold values from -0.125 to 0.125
- w_up: bfloat16 [16, 768, 2048], P(('ctx', 'exp'), None, 'head'), may hold values from -0.125 to 0.125
- w_down: bfloat16 [16, 768, 2048], P(('ctx', 'exp'), None, 'head'), may hold values from -0.21875 to 0.21875
- cotangent: bfloat16 [1024, 2048], P(('ctx', 'exp')), may hold values from -6 to 6
Outputs:
- layer_out: bfloat16 [1024, 2048], P(('ctx', 'exp'), 'head')
- grad_gate: bfloat16 [16, 768, 2048], P(('ctx', 'exp'), None, 'head')
- grad_up: bfloat16 [16, 768, 2048], P(('ctx', 'exp'), None, 'head')
- grad_down: bfloat16 [16, 768, 2048], P(('ctx', 'exp'), None, 'head')
Inputs may be any that keep to these rules, and one draw needn't show every extreme that they name: `routes`: in the rows of one index of ctx+exp (aligned blocks of 128 rows) no expert is named more than 80 times, a bound that some block reaches; a row names 8 different experts. `doc_ids`: ids never fall along positions; a document spans 1 to 768 positions, one exactly 768.
All inputs are finite; a program needn't handle non-finite values.
Results may differ from a plain program's by a relative error of at most 0.018.
Values may be sent and summed in bfloat16 or wider, within the bound.
A program may use at most 128 MiB of HBM per device.

v0:
```python
import math

import jax
import jax.numpy as jnp
from jax import lax
from jax.sharding import PartitionSpec as P

HEAD_DIMENSION = 128


def attend_block(
    query_block, key_rows, value_rows, query_doc, key_doc, query_pos, key_pos, score_scale
):
    scores = (
        jnp.einsum("tgrd,sgd->gtrs", query_block, key_rows, preferred_element_type=jnp.float32)
        * score_scale
    )
    visible = (key_pos[None, :] <= query_pos[:, None]) & (key_doc[None, :] == query_doc[:, None])
    visible = visible[None, :, None, :]
    scores = jnp.where(visible, scores, -1e30)
    row_max = jnp.max(scores, axis=-1, keepdims=True)
    weights = jnp.where(visible, jnp.exp(scores - row_max), 0.0)
    row_total = jnp.sum(weights, axis=-1)
    mixed = jnp.einsum(
        "gtrs,sgd->tgrd",
        weights.astype(jnp.bfloat16),
        value_rows,
        preferred_element_type=jnp.float32,
    )
    return (mixed / jnp.transpose(row_total, (1, 0, 2))[..., None]).astype(jnp.bfloat16)


def forward_share(gate_share, up_share):
    sigma = jax.nn.sigmoid(gate_share)
    silu_gate = gate_share * sigma
    return (sigma, silu_gate, (silu_gate * up_share).astype(jnp.bfloat16))


def backward_share(grad_share, gate_share, up_share, sigma, silu_gate):
    gate_grad = (grad_share * up_share * sigma * (1.0 + gate_share * (1.0 - sigma))).astype(
        jnp.bfloat16
    )
    up_grad = (grad_share * silu_gate).astype(jnp.bfloat16)
    return (gate_grad, up_grad)


def per_device(
    resid,
    queries,
    rotated_key_value_pairs,
    doc_ids,
    out_weight,
    norm_gain,
    routes,
    probs,
    w_gate,
    w_up,
    w_down,
    cotangent,
):
    tok_rows, model_width = resid.shape
    top_count = routes.shape[1]
    exp_dev = w_gate.shape[0]
    n_ctx = lax.axis_size("ctx")
    n_exp = lax.axis_size("exp")
    n_head = lax.axis_size("head")
    owners = n_ctx * n_exp
    experts = exp_dev * owners
    capacity = max(2, tok_rows * top_count * 5 // (4 * experts))
    head_size = HEAD_DIMENSION
    kv_local = rotated_key_value_pairs.shape[2] // head_size
    group_width = queries.shape[1] // (head_size * kv_local)
    whole_kv, whole_doc = (
        lax.all_gather(rotated_key_value_pairs, ("ctx", "exp"), axis=1, tiled=True),
        lax.all_gather(doc_ids, ("ctx", "exp"), axis=1, tiled=True),
    )
    total_rows = whole_kv.shape[1]
    key_rows = whole_kv[0].reshape(total_rows, kv_local, head_size)
    value_rows = whole_kv[1].reshape(total_rows, kv_local, head_size)
    key_doc = whole_doc[0]
    key_pos = jnp.arange(total_rows, dtype=jnp.int32)
    query_pos = lax.axis_index(("ctx", "exp")) * tok_rows + jnp.arange(tok_rows, dtype=jnp.int32)
    query_doc = doc_ids[0]
    group_step = math.gcd(group_width, max(1, 512 // tok_rows))
    block_count = group_width // group_step
    query_blocks = jnp.moveaxis(
        queries.reshape(tok_rows, kv_local, block_count, group_step, head_size), 2, 0
    )
    score_scale = head_size ** (-0.5)

    def attend_one(query_block):
        return attend_block(
            query_block, key_rows, value_rows, query_doc, key_doc, query_pos, key_pos, score_scale
        )

    attn = lax.map(attend_one, query_blocks)
    attn = jnp.moveaxis(attn, 0, 2).reshape(tok_rows, -1)
    partial_value = jnp.dot(
        attn,
        lax.all_gather(out_weight, ("ctx", "exp"), axis=1, tiled=True),
        preferred_element_type=jnp.float32,
    )
    attn_sum = lax.psum(partial_value, "head")
    hidden_state = (resid.astype(jnp.float32) + attn_sum).astype(jnp.bfloat16)
    hstate = hidden_state.astype(jnp.float32)
    inverse = lax.rsqrt(jnp.mean(hstate * hstate, axis=-1, keepdims=True) + 1e-06)
    normed = (hstate * inverse * norm_gain).astype(jnp.bfloat16)
    flat_routes = routes.reshape(-1)
    assigned = flat_routes.shape[0]
    onehot = (flat_routes[:, None] == jnp.arange(experts, dtype=jnp.int32)[None, :]).astype(
        jnp.int32
    )
    slot_rank = jnp.sum((jnp.cumsum(onehot, axis=0) - onehot) * onehot, axis=1)
    slot_index = flat_routes * capacity + slot_rank
    slot_owner = jnp.full((experts * capacity,), assigned, jnp.int32)
    slot_owner = slot_owner.at[slot_index].set(jnp.arange(assigned, dtype=jnp.int32))
    slot_rows = slot_owner // top_count
    flat_probs = probs.reshape(-1)
    probs_pad = jnp.concatenate([flat_probs, jnp.zeros((1,), jnp.float32)])
    head_index = lax.axis_index("head")
    quarter = model_width // n_head
    source_rows = lax.dynamic_slice_in_dim(normed, head_index * quarter, quarter, 1)
    source_cot = lax.dynamic_slice_in_dim(cotangent, head_index * quarter, quarter, 1)
    rows_pad = jnp.concatenate([source_rows, jnp.zeros((1, quarter), jnp.bfloat16)], axis=0)
    cot_pad = jnp.concatenate([source_cot, jnp.zeros((1, quarter), jnp.bfloat16)], axis=0)
    send_rows = rows_pad[slot_rows].reshape(owners, exp_dev * capacity, quarter)
    send_grads = (probs_pad[slot_owner][:, None] * cot_pad[slot_rows].astype(jnp.float32)).astype(
        jnp.bfloat16
    )
    send_grads = send_grads.reshape(owners, exp_dev * capacity, quarter)
    got_rows, got_grads = (
        lax.all_to_all(
            lax.all_to_all(
                send_rows.reshape(n_ctx, n_exp, exp_dev * capacity, quarter),
                "ctx",
                split_axis=0,
                concat_axis=0,
                tiled=True,
            ),
            "exp",
            split_axis=1,
            concat_axis=1,
            tiled=True,
        ),
        lax.all_to_all(
            lax.all_to_all(
                send_grads.reshape(n_ctx, n_exp, exp_dev * capacity, quarter),
                "ctx",
                split_axis=0,
                concat_axis=0,
                tiled=True,
            ),
            "exp",
            split_axis=1,
            concat_axis=1,
            tiled=True,
        ),
    )
    slot_inputs = got_rows.reshape(owners, exp_dev, capacity, quarter)
    slot_grads = got_grads.reshape(owners, exp_dev, capacity, quarter)
    gate_part = jnp.einsum(
        "secd,efd->secf", slot_inputs, w_gate, preferred_element_type=jnp.float32
    )
    up_part = jnp.einsum("secd,efd->secf", slot_inputs, w_up, preferred_element_type=jnp.float32)
    grad_part = jnp.einsum("secd,efd->secf", slot_grads, w_down, preferred_element_type=jnp.float32)
    gate_share, up_share = (
        lax.psum_scatter(gate_part, "head", scatter_dimension=3, tiled=True),
        lax.psum_scatter(up_part, "head", scatter_dimension=3, tiled=True),
    )
    sigma, silu_gate, hidden_share = forward_share(gate_share, up_share)
    hidden = lax.all_gather(hidden_share, "head", axis=3, tiled=True)
    grad_share = lax.psum_scatter(grad_part, "head", scatter_dimension=3, tiled=True)
    gate_grad_share, up_grad_share = backward_share(
        grad_share, gate_share, up_share, sigma, silu_gate
    )
    gate_grad, up_grad = (
        lax.all_gather(gate_grad_share, "head", axis=3, tiled=True),
        lax.all_gather(up_grad_share, "head", axis=3, tiled=True),
    )
    expert_out = jnp.einsum(
        "secf,efd->secd", hidden, w_down, preferred_element_type=jnp.float32
    ).astype(jnp.bfloat16)
    grad_down = jnp.einsum(
        "secf,secd->efd", hidden, slot_grads, preferred_element_type=jnp.float32
    ).astype(jnp.bfloat16)
    grad_gate = jnp.einsum(
        "secf,secd->efd", gate_grad, slot_inputs, preferred_element_type=jnp.float32
    ).astype(jnp.bfloat16)
    grad_up = jnp.einsum(
        "secf,secd->efd", up_grad, slot_inputs, preferred_element_type=jnp.float32
    ).astype(jnp.bfloat16)
    returned = lax.all_to_all(
        expert_out.reshape(owners, exp_dev * capacity, quarter),
        ("ctx", "exp"),
        split_axis=0,
        concat_axis=0,
        tiled=True,
    )
    returned = returned.reshape(experts * capacity, quarter)
    picked = returned[slot_index].astype(jnp.float32) * flat_probs[:, None]
    moe_part = jnp.sum(picked.reshape(tok_rows, top_count, quarter), axis=1)
    own_state = lax.dynamic_slice_in_dim(hstate, head_index * quarter, quarter, 1)
    layer_out = (own_state + moe_part).astype(jnp.bfloat16)
    return (layer_out, grad_gate, grad_up, grad_down)


def solution(mesh):
    return jax.shard_map(
        per_device,
        mesh=mesh,
        in_specs=(
            P(("ctx", "exp"), None),
            P(("ctx", "exp"), "head"),
            P(None, ("ctx", "exp"), "head"),
            P(None, ("ctx", "exp")),
            P("head", ("ctx", "exp")),
            P(),
            P(("ctx", "exp"), None),
            P(("ctx", "exp"), None),
            P(("ctx", "exp"), None, "head"),
            P(("ctx", "exp"), None, "head"),
            P(("ctx", "exp"), None, "head"),
            P(("ctx", "exp"), None),
        ),
        out_specs=(
            P(("ctx", "exp"), "head"),
            P(("ctx", "exp"), None, "head"),
            P(("ctx", "exp"), None, "head"),
            P(("ctx", "exp"), None, "head"),
        ),
        check_vma=False,
    )
```

profile of v0, /device:TPU:9, one launch (start us, length us, event | category | flops | bytes accessed | tf_op | source)
XLA Modules:
  0.0 437.9 jit_solution(17681612106845468307)
XLA Ops:
  11.2 4.5 %reduce-window.6 = s32[16,8,128]{2,1,0:T(8,128)S(1)} reduce-window(s32[16,8,128]{2,1,0:T(8,128)S(1)} %fusion.64, s32[]{:T(128)} %copy.170), window={size=1x1x128 pad=0_0x0_0x127_0}, to_apply=%region_6.7 | reduce-window | flops 2080768 | bytes 131076 | tf_op jit(solution)/shard_map/reduce-window
  16.2 4.3 scatter_custom_fusion
  20.6 7.1 %gather_fusion.2 = f32[1280]{0:T(1024)S(1)} fusion(f32[1025]{0:T(1024)S(1)} %pad_maximum_fusion, s32[2048]{0:T(1024)S(1)} %get-tuple-element.131), kind=kCustom, calls=%fused_computation.2 | custom fusion | bytes 15360 | tf_op jit(solution)/shard_map/gather | solution.py:127
  28.7 4.1 gather_fusion.3
  34.2 3.8 all-to-all-start.3
  38.2 13.7 %all_gather.18 = s32[1,1024]{1,0:T(1,128)S(1)} all-gather(s32[1,128]{1,0:T(1,128)S(1)} %copy-done.11), channel_id=1, replica_groups=mesh['ctx'=2,'head'=4,'exp'=4] {'ctx','exp'}, dimensions={1}, use_global_device_ids=true | all-gather | bytes 4608 | tf_op jit(solution)/shard_map/all_gather | solution.py:75
  51.9 31.2 %all_gather.19 = bf16[2,1024,128]{2,1,0:T(8,128)(2,1)S(1)} all-gather(bf16[2,128,128]{2,1,0:T(8,128)(2,1)S(1)} %copy-done.10), channel_id=1, replica_groups=mesh['ctx'=2,'head'=4,'exp'=4] {'ctx','exp'}, dimensions={1}, use_global_device_ids=true | all-gather | bytes 589824 | tf_op jit(solution)/shard_map/all_gather | solution.py:74
  85.1 6.2 %all-to-all-start.4 = ((bf16[2,4,160,512]{3,2,0,1:T(8,128)(2,1)}), bf16[2,4,160,512]{3,2,0,1:T(8,128)(2,1)S(1)}, u32[]{:S(2)}, u32[]{:S(2)}) async-start(bf16[2,4,160,512]{3,2,0,1:T(8,128)(2,1)} %copy.110), calls=%async_computation.4 | async-start | bytes 2621440 | tf_op jit(solution)/shard_map/all_to_all | solution.py:145
  91.3 11.4 %while.11 = (s32[]{:T(128)}, bf16[2,128,1,4,128]{1,4,3,0,2:T(8,128)(2,1)}, s32[1,1024]{1,0:T(1,128)S(1)}, s32[1,128]{1,0:T(1,128)S(1)}, bf16[2,128,1,4,128]{1,4,...) while((s32[]{:T(128)}, ...), condition=%wide.region_3.4_spmd.clone, body=%wide.region_0.3_spmd.clone.sunk | while | flops 272106624 | bytes 3810929 | solution.py:96
  102.8 4.0 fusion.75
  106.8 4.3 all-to-all-done.4
  115.5 6.1 %copy.131 = f32[8,2,80,768]{2,0,1,3:T(8,128)} copy(f32[8,2,80,768]{3,2,0,1:T(8,128)} %convolution_bitcast_fusion.1) | data formatting | bytes 7864320
  121.5 7.2 %reshape.259 = f32[768,1280]{1,0:T(8,128)} reshape(f32[768,2,8,80]{3,2,1,0:T(8,128)} %bitcast.157) | data formatting | bytes 7864320
  129.6 23.5 %all-reduce.4.cloned.1.call-done = f32[128,2048]{1,0:T(8,128)} async-done(((f32[128,2048]{1,0:T(8,128)}), f32[128,2048]{1,0:T(8,128)}) %all-reduce.4.cloned.1.call-update) | async-done | bytes 1048592 | tf_op jit(solution)/shard_map/psum | solution.py:103
  155.6 4.1 gather_fusion
  159.7 17.7 %all_to_all.25 = bf16[2,4,160,512]{3,2,1,0:T(8,128)(2,1)S(1)} all-to-all(bf16[2,4,160,512]{3,2,1,0:T(8,128)(2,1)S(1)} %bitcast.168), channel_id=1, replica_groups=mesh['ctx'=2,'head'=4,'exp'=4] {'ctx'}, dimensions={0} | all-to-all | bytes 2621440 | tf_op jit(solution)/shard_map/all_to_all | solution.py:133
  177.5 32.7 %all_to_all.26 = bf16[2,4,160,512]{3,2,0,1:T(8,128)(2,1)S(1)} all-to-all(bf16[2,4,160,512]{3,2,0,1:T(8,128)(2,1)S(1)} %copy.101), channel_id=1, replica_groups=mesh['ctx'=2,'head'=4,'exp'=4] {'exp'}, dimensions={1} | all-to-all | bytes 2621440 | tf_op jit(solution)/shard_map/all_to_all | solution.py:132
  215.3 6.1 %copy.129 = f32[8,2,80,768]{2,0,1,3:T(8,128)} copy(f32[8,2,80,768]{3,2,0,1:T(8,128)} %convolution_bitcast_fusion.2) | data formatting | bytes 7864320
  221.3 7.2 %reshape.257 = f32[768,1280]{1,0:T(8,128)} reshape(f32[768,2,8,80]{3,2,1,0:T(8,128)} %bitcast.158) | data formatting | bytes 7864320
  228.6 4.5 %convolution_bitcast_fusion.3 = f32[8,2,80,768]{3,2,0,1:T(8,128)} fusion(bf16[2,768,512]{2,1,0:T(8,128)(2,1)} %param.22, bf16[8,2,80,512]{3,2,1,0:T(8,128)(2,1)S(1)} %bitcast.161), kind=kOutput, calls=%fused_computation.47 | convolution fusion | flops 1006632960 | bytes 6815744 | tf_op jit(solution)/shard_map/secd,efd->secf/dot_general | solution.py:161
  233.1 6.2 %copy.127 = f32[8,2,80,768]{2,0,1,3:T(8,128)} copy(f32[8,2,80,768]{3,2,0,1:T(8,128)} %convolution_bitcast_fusion.3) | data formatting | bytes 7864320
  239.3 7.5 %reshape.255 = f32[768,1280]{1,0:T(8,128)} reshape(f32[768,2,8,80]{3,2,1,0:T(8,128)} %bitcast.159) | data formatting | bytes 7864320
  250.9 22.1 %reduce-scatter.12.cloned.1.call-done = f32[192,1280]{1,0:T(8,128)} async-done(((f32[768,1280]{1,0:T(8,128)}), f32[192,1280]{1,0:T(8,128)}) %reduce-scatter.12.cloned.1.call-update) | async-done | bytes 983056
  277.0 41.5 %reduce-scatter.10.cloned.1.call-done = f32[192,1280]{1,0:T(8,128)} async-done(((f32[768,1280]{1,0:T(8,128)}), f32[192,1280]{1,0:T(8,128)}) %reduce-scatter.10.cloned.1.call-update) | async-done | bytes 983056
  330.1 25.8 %all-gather.7.cloned.1.call-done = bf16[8,2,80,768]{2,0,1,3:T(8,128)(2,1)} async-done(((bf16[8,2,80,192]{2,0,1,3:T(8,128)(2,1)}), bf16[8,2,80,768]{2,0,1,3:T(8,128)(2,1)}) %all-gather.7.cloned.1.call-update) | async-done | bytes 1966096 | tf_op jit(solution)/shard_map/all_gather | solution.py:171
  362.2 5.5 %all-to-all-start.2 = ((bf16[8,160,512]{2,1,0:T(8,128)(2,1)}), bf16[8,160,512]{2,1,0:T(8,128)(2,1)S(1)}, u32[]{:S(2)}, u32[]{:S(2)}) async-start(bf16[8,160,512]{2,1,0:T(8,128)(2,1)} %bitcast.169), calls=%async_computation.2 | async-start | bytes 2621440 | tf_op jit(solution)/shard_map/all_to_all | solution.py:192
  367.7 4.5 %bitcast_convert_fusion = bf16[2,768,512]{2,1,0:T(8,128)(2,1)} fusion(bf16[8,2,80,768]{3,2,0,1:T(8,128)(2,1)} %copy-done.4, bf16[8,2,80,512]{3,2,1,0:T(8,128)(2,1)} %bitcast.171), kind=kOutput, calls=%fused_computation.34 | convolution fusion | flops 1007419392 | bytes 4849664 | tf_op jit(solution)/shard_map/secf,secd->efd/dot_general | solution.py:183
  372.1 14.5 %all-gather.11.cloned.1.call-done = bf16[8,2,80,768]{2,0,1,3:T(8,128)(2,1)} async-done(((bf16[8,2,80,192]{2,0,1,3:T(8,128)(2,1)}), bf16[8,2,80,768]{2,0,1,3:T(8,128)(2,1)}) %all-gather.11.cloned.1.call-update) | async-done | bytes 1966096 | tf_op jit(solution)/shard_map/all_gather | solution.py:178
  386.6 5.1 %bitcast_convert_fusion.1 = bf16[2,768,512]{2,1,0:T(8,128)(2,1)} fusion(bf16[8,2,80,768]{2,0,1,3:T(8,128)(2,1)} %all-gather.11.cloned.1.call-done, bf16[8,2,80,512]{3,2,1,0:T(8,128)(2,1)} %bitcast.162), kind=kOutput, calls=%fused_computation.35 | convolution fusion | flops 1007419392 | bytes 4849664 | tf_op jit(solution)/shard_map/secf,secd->efd/dot_general | solution.py:189
  391.7 25.6 %all-gather.9.cloned.1.call-done = bf16[8,2,80,768]{2,0,1,3:T(8,128)(2,1)} async-done(((bf16[8,2,80,192]{2,0,1,3:T(8,128)(2,1)}), bf16[8,2,80,768]{2,0,1,3:T(8,128)(2,1)}) %all-gather.9.cloned.1.call-update) | async-done | bytes 1966096 | tf_op jit(solution)/shard_map/all_gather | solution.py:177
  417.3 5.1 %bitcast_convert_fusion.2 = bf16[2,768,512]{2,1,0:T(8,128)(2,1)} fusion(bf16[8,2,80,768]{2,0,1,3:T(8,128)(2,1)} %all-gather.9.cloned.1.call-done, bf16[8,2,80,512]{3,2,1,0:T(8,128)(2,1)} %bitcast.163), kind=kOutput, calls=%fused_computation.36 | convolution fusion | flops 1007419392 | bytes 4849664 | tf_op jit(solution)/shard_map/secf,secd->efd/dot_general | solution.py:186
  422.4 5.1 %gather_fusion.1 = bf16[1024,512]{1,0:T(8,128)(2,1)} fusion(bf16[1280,512]{1,0:T(8,128)(2,1)S(1)} %bitcast.156, s32[1024]{0:T(1024)S(1)} %broadcast_clamp_fusion), kind=kCustom, calls=%fused_computation.1 | custom fusion | bytes 2101248 | tf_op jit(solution)/shard_map/gather | solution.py:200
  (111 shorter events, 62.9 us)
Async XLA Ops:
  7.2 105.1 %copy-start = (bf16[2,768,512]{2,1,0:T(8,128)(2,1)S(1)}, bf16[2,768,512]{2,1,0:T(8,128)(2,1)}, u32[]{:S(2)}) copy-start(bf16[2,768,512]{2,1,0:T(8,128)(2,1)} %param.24) | copy-start | bytes 4718596
  7.2 95.6 %all-gather.5.cloned.1.call-start = ((), (), s32[]{:S(2)}) async-start(), calls=%async_computation.8 | async-start | bytes 4718592 | tf_op jit(solution)/shard_map/all_gather | solution.py:100
  10.6 0.6 copy-start.6
  34.2 3.8 copy-start.9
  34.2 4.0 copy-start.11
  34.2 17.7 %copy-start.10 = (bf16[2,128,128]{2,1,0:T(8,128)(2,1)S(1)}, bf16[2,128,128]{2,1,0:T(8,128)(2,1)}, u32[]{:S(2)}) copy-start(bf16[2,128,128]{2,1,0:T(8,128)(2,1)} %param.16) | copy-start | bytes 196612
  34.2 49.7 %all-to-all-start.3 = ((bf16[2,4,160,512]{3,2,1,0:T(8,128)(2,1)}), bf16[2,4,160,512]{3,2,1,0:T(8,128)(2,1)S(1)}, u32[]{:S(2)}, u32[]{:S(2)}) async-start(bf16[2,4,160,512]{3,2,1,0:T(8,128)(2,1)} %fusion.40), calls=%async_computation.3 | async-start | bytes 2621440 | tf_op jit(solution)/shard_map/all_to_all | solution.py:146
  85.1 25.9 %all-to-all-start.4 = ((bf16[2,4,160,512]{3,2,0,1:T(8,128)(2,1)}), bf16[2,4,160,512]{3,2,0,1:T(8,128)(2,1)S(1)}, u32[]{:S(2)}, u32[]{:S(2)}) async-start(bf16[2,4,160,512]{3,2,0,1:T(8,128)(2,1)} %copy.110), calls=%async_computation.4 | async-start | bytes 2621440 | tf_op jit(solution)/shard_map/all_to_all | solution.py:145
  91.3 61.8 %all-reduce.4.cloned.1.call-start = ((), (), s32[]{:S(2)}) async-start(), calls=%async_computation.9 | async-start | bytes 2097152 | tf_op jit(solution)/shard_map/psum | solution.py:103
  106.8 140.1 %reduce-scatter.14.cloned.1.call-start = ((), (), s32[]{:S(2)}) async-start(), calls=%async_computation.15 | async-start | bytes 4915200
  111.2 1.1 copy-start.2
  128.8 24.4 %copy-start.8 = (bf16[128,2048]{1,0:T(8,128)(2,1)S(1)}, bf16[128,2048]{1,0:T(8,128)(2,1)}, u32[]{:S(2)}) copy-start(bf16[128,2048]{1,0:T(8,128)(2,1)} %param.14) | copy-start | bytes 1572868
  128.8 144.2 %reduce-scatter.12.cloned.1.call-start = ((), (), s32[]{:S(2)}) async-start(), calls=%async_computation.14 | async-start | bytes 4915200
  154.6 1.0 copy-start.3
  210.2 1.9 copy-start.5
  210.3 18.3 %copy-start.1 = (bf16[2,4,160,512]{3,2,1,0:T(8,128)(2,1)}, bf16[2,4,160,512]{3,2,1,0:T(8,128)(2,1)S(1)}, u32[]{:S(2)}) copy-start(bf16[2,4,160,512]{3,2,1,0:T(8,128)(2,1)S(1)} %copy.102) | copy-start | bytes 3932164
  228.6 89.9 %reduce-scatter.10.cloned.1.call-start = ((), (), s32[]{:S(2)}) async-start(), calls=%async_computation.13 | async-start | bytes 4915200
  246.8 109.1 %all-gather.7.cloned.1.call-start = ((), (), s32[]{:S(2)}) async-start(), calls=%async_computation.10 | async-start | bytes 3932160 | tf_op jit(solution)/shard_map/all_gather | solution.py:171
  326.8 59.8 %all-gather.11.cloned.1.call-start = ((), (), s32[]{:S(2)}) async-start(), calls=%async_computation.12 | async-start | bytes 3932160 | tf_op jit(solution)/shard_map/all_gather | solution.py:178
  328.6 88.7 %all-gather.9.cloned.1.call-start = ((), (), s32[]{:S(2)}) async-start(), calls=%async_computation.11 | async-start | bytes 3932160 | tf_op jit(solution)/shard_map/all_gather | solution.py:177
  359.6 1.3 copy-start.4
  362.2 60.2 %all-to-all-start.2 = ((bf16[8,160,512]{2,1,0:T(8,128)(2,1)}), bf16[8,160,512]{2,1,0:T(8,128)(2,1)S(1)}, u32[]{:S(2)}, u32[]{:S(2)}) async-start(bf16[8,160,512]{2,1,0:T(8,128)(2,1)} %bitcast.169), calls=%async_computation.2 | async-start | bytes 2621440 | tf_op jit(solution)/shard_map/all_to_all | solution.py:192
  422.4 5.1 %copy-start.7 = (f32[128,8]{1,0:T(8,128)S(1)}, f32[128,8]{1,0:T(8,128)}, u32[]{:S(2)}) copy-start(f32[128,8]{1,0:T(8,128)} %copy-done.6) | copy-start | bytes 12292
Sparse Core Ops, SparseCore 0:
  10.0 87.0 all-gather.4
  106.9 46.1 all-reduce.3
  155.8 43.7 reduce-scatter.13
  228.7 44.2 reduce-scatter.11
  275.5 42.8 reduce-scatter.9
  326.9 28.9 all-gather.6
  358.0 28.5 all-gather.10
  388.7 28.5 all-gather.8
where the time goes:
time: 441 us; the launch traced here: 438 us
  waiting for transfers between devices  158 us (36%)
  local copies, waits for them, and re-layouts  98.8 us (22%)
  blocking collectives  95.3 us (22%)
  matrix products  40.1 us (9%)
  starting transfers between devices  15.9 us (4%)
  other arithmetic  15.2 us (3%)
  between operations  14.5 us (3%)
    unnamed x11, waiting for transfers between devices  64.4 us
    unnamed x39, local copies, waits for them, and re-layouts  58.2 us
    all_to_all x1, blocking collectives, per_device(): lax.all_to_all(lax.all_to_all(send_rows.reshape(n_ctx, n_exp, exp_dev * c...  32.7 us
    all_gather x1, blocking collectives, per_device(): lax.all_gather(rotated_key_value_pairs, ('ctx', 'exp'), axis=1, tiled=True)  31.2 us
    all_gather x1, waiting for transfers between devices, per_device(): hidden = lax.all_gather(hidden_share, 'head', axis=3, tiled=True)  25.8 us
    all_gather x1, waiting for transfers between devices, per_device(): lax.all_gather(gate_grad_share, 'head', axis=3, tiled=True)  25.6 us
    psum x1, waiting for transfers between devices, per_device(): attn_sum = lax.psum(partial_value, 'head')  23.5 us
    all_to_all x1, blocking collectives, per_device(): lax.all_to_all(send_rows.reshape(n_ctx, n_exp, exp_dev * capacity, quarte...  17.7 us
  transfers between devices with their start and end apart: 11, of which 7 were waited for; matrix products, arithmetic and copies ran while one was open for 30% of the time, Pallas kernels for 0%

commit v1 on v0

--- a/solution.py
+++ b/solution.py
@@ -1,9 +1,16 @@
+import functools
 import math
 
 import jax
 import jax.numpy as jnp
 from jax import lax
+from jax.experimental import pallas as pl
+from jax.experimental.pallas import tpu as pltpu
 from jax.sharding import PartitionSpec as P
+
+MESH = pl.DeviceIdType.MESH
+BF16 = jnp.bfloat16
+F32 = jnp.float32
 
 HEAD_DIMENSION = 128
 
@@ -44,7 +51,7 @@
     return (gate_grad, up_grad)
 
 
-def per_device(
+def per_device_slots(
     resid,
     queries,
     rotated_key_value_pairs,
@@ -204,6 +211,603 @@
     return (layer_out, grad_gate, grad_up, grad_down)
 
 
+def ring_id(ctx, head, exp):
+    return {"ctx": ctx, "head": head, "exp": exp}
+
+
+def remote(src, dst, send_sem, recv_sem, device):
+    return pltpu.make_async_remote_copy(
+        src_ref=src,
+        dst_ref=dst,
+        send_sem=send_sem,
+        recv_sem=recv_sem,
+        device_id=device,
+        device_id_type=MESH,
+    )
+
+
+def greet(devices):
+    barrier = pltpu.get_barrier_semaphore()
+    for device in devices:
+        pl.semaphore_signal(barrier, inc=1, device_id=device, device_id_type=MESH)
+    pl.semaphore_wait(barrier, len(devices))
+
+
+def token_group(n_exp):
+    ctx, head, exp = lax.axis_index("ctx"), lax.axis_index("head"), lax.axis_index("exp")
+    others = []
+    for dx in range(2):
+        for dz in range(n_exp):
+            if dx or dz:
+                to_ctx = 1 - ctx if dx else ctx
+                to_exp = lax.rem(exp + dz, n_exp)
+                from_exp = lax.rem(exp + n_exp - dz, n_exp)
+                others.append(
+                    (dx * n_exp + dz, ring_id(to_ctx, head, to_exp), to_ctx * n_exp + to_exp,
+                     to_ctx * n_exp + from_exp)
+                )
+    return others
+
+
+class Gather:
+    def __init__(self, n_exp, own, block, send_sem, recv_sem):
+        self.n_exp, self.own, self.block = n_exp, own, block
+        self.send_sem, self.recv_sem = send_sem, recv_sem
+        self.ctx, self.head = lax.axis_index("ctx"), lax.axis_index("head")
+        self.exp = lax.axis_index("exp")
+        self.me = self.ctx * n_exp + self.exp
+        self.across = ring_id(1 - self.ctx, self.head, self.exp)
+        self.sent = []
+
+    def start(self):
+        for dz in range(1, self.n_exp):
+            device = ring_id(self.ctx, self.head, lax.rem(self.exp + dz, self.n_exp))
+            self.send(self.own, self.me, dz, device)
+        self.send(self.own, self.me, self.n_exp, self.across)
+
+    def send(self, source, index, sem, device):
+        copy = remote(
+            source, self.block(index), self.send_sem.at[sem], self.recv_sem.at[sem], device
+        )
+        copy.start()
+        self.sent.append(copy)
+
+    def arrived(self, index, sem):
+        remote(
+            self.block(index),
+            self.block(index),
+            self.send_sem.at[sem],
+            self.recv_sem.at[sem],
+            self.across,
+        ).wait_recv()
+
+    def forward(self):
+        for dz in range(1, self.n_exp):
+            index = self.ctx * self.n_exp + lax.rem(self.exp + self.n_exp - dz, self.n_exp)
+            self.arrived(index, dz)
+            self.send(self.block(index), index, self.n_exp + dz, self.across)
+
+    def finish(self):
+        other = (1 - self.ctx) * self.n_exp
+        self.arrived(other + self.exp, self.n_exp)
+        for dz in range(1, self.n_exp):
+            self.arrived(
+                other + lax.rem(self.exp + self.n_exp - dz, self.n_exp), self.n_exp + dz
+            )
+        for copy in self.sent:
+            copy.wait_send()
+
+
+def attention_kernel(
+    n_exp,
+    heads,
+    kv_ref,
+    query_ref,
+    doc_ref,
+    meta_ref,
+    cot_ref,
+    attn_ref,
+    cot_all,
+    meta_all,
+    kv_all,
+    meta_send,
+    meta_recv,
+    kv_send,
+    kv_recv,
+    cot_send,
+    cot_recv,
+):
+    rows, quarter = cot_all.shape[1:]
+    me = lax.axis_index("ctx") * n_exp + lax.axis_index("exp")
+    others = token_group(n_exp)
+    greet([device for _, device, _, _ in others])
+
+    def kv_block(index):
+        return kv_all.at[:, pl.ds(pl.multiple_of(index * rows, rows), rows), :]
+
+    kv_gather = Gather(n_exp, kv_ref, kv_block, kv_send, kv_recv)
+    kv_gather.start()
+    meta_copies = []
+    for sem, device, to_block, _ in others:
+        copy = remote(
+            meta_ref.at[to_block], meta_all.at[me], meta_send.at[sem], meta_recv.at[sem], device
+        )
+        copy.start()
+        meta_copies.append(copy)
+    kv_all[:, pl.ds(pl.multiple_of(me * rows, rows), rows), :] = kv_ref[...]
+    meta_all[me] = meta_ref[me]
+    column = pl.multiple_of(lax.axis_index("head") * quarter, quarter)
+    own_cot = cot_ref.at[:, pl.ds(column, quarter)]
+    kv_gather.forward()
+    cot_gather = Gather(n_exp, own_cot, lambda index: cot_all.at[index], cot_send, cot_recv)
+    cot_gather.start()
+    cot_all[me] = cot_ref[:, pl.ds(column, quarter)]
+    kv_gather.finish()
+    for sem, device, _, from_block in others:
+        remote(
+            meta_all.at[from_block],
+            meta_all.at[from_block],
+            meta_send.at[sem],
+            meta_recv.at[sem],
+            device,
+        ).wait_recv()
+    for copy in meta_copies:
+        copy.wait_send()
+
+    total = kv_all.shape[1]
+    key_doc = jnp.concatenate([meta_all[s, 2:3, :] for s in range(total // rows)], axis=1)
+    key_pos = lax.broadcasted_iota(jnp.int32, (rows, total), 1)
+    query_pos = me * rows + lax.broadcasted_iota(jnp.int32, (rows, total), 0)
+    visible = (key_pos <= query_pos) & (key_doc == doc_ref[:, 0:1])
+    scale = HEAD_DIMENSION ** (-0.5)
+    for head in range(heads):
+        lanes = slice(head * HEAD_DIMENSION, (head + 1) * HEAD_DIMENSION)
+        scores = lax.dot_general(
+            query_ref[:, lanes], kv_all[0], (((1,), (1,)), ((), ())), preferred_element_type=F32
+        )
+        scores = jnp.where(visible, scores * scale, -1e30)
+        weights = jnp.exp(scores - jnp.max(scores, axis=1, keepdims=True))
+        row_total = jnp.sum(weights, axis=1, keepdims=True)
+        mixed = jnp.dot(weights.astype(BF16), kv_all[1], preferred_element_type=F32)
+        attn_ref[:, lanes] = (mixed / row_total).astype(BF16)
+        if head == heads // 2:
+            cot_gather.forward()
+    cot_gather.finish()
+
+
+def norm_kernel(
+    n_exp,
+    attn_ref,
+    weight_ref,
+    resid_ref,
+    gain_ref,
+    state_ref,
+    normed_all,
+    part_out,
+    part_in,
+    square_out,
+    square_in,
+    own_normed,
+    part_send,
+    part_recv,
+    square_send,
+    square_recv,
+    token_send,
+    token_recv,
+):
+    ctx, head, exp = lax.axis_index("ctx"), lax.axis_index("head"), lax.axis_index("exp")
+    me = ctx * n_exp + exp
+    rows, quarter = state_ref.shape
+    width = resid_ref.shape[1]
+    peers = {r: ring_id(ctx, head ^ r, exp) for r in (1, 2, 3)}
+    along = [ring_id(ctx, head, lax.rem(exp + dz, n_exp)) for dz in range(1, n_exp)]
+    greet([peers[r] for r in (1, 2, 3)] + along + [ring_id(1 - ctx, head, exp)])
+
+    def partial(index):
+        columns = pl.ds(pl.multiple_of(index * quarter, quarter), quarter)
+        return jnp.dot(attn_ref[...], weight_ref[:, columns], preferred_element_type=F32)
+
+    copies = []
+    for r in (2, 3, 1):
+        part_out[r - 1] = partial(head ^ r).astype(BF16)
+        copy = remote(
+            part_out.at[r - 1],
+            part_in.at[r - 1],
+            part_send.at[r - 1],
+            part_recv.at[r - 1],
+            peers[r],
+        )
+        copy.start()
+        copies.append(copy)
+    columns = pl.ds(pl.multiple_of(head * quarter, quarter), quarter)
+    state = partial(head)
+    for copy in copies:
+        copy.wait_recv()
+    for r in range(3):
+        state = state + part_in[r].astype(F32)
+    state = (resid_ref[:, columns].astype(F32) + state).astype(BF16)
+    state_ref[...] = state
+    state = state.astype(F32)
+    squares = jnp.sum(state * state, axis=1, keepdims=True)
+    square_out[...] = jnp.broadcast_to(squares, square_out.shape)
+    square_copies = []
+    for r in (2, 3, 1):
+        copy = remote(
+            square_out,
+            square_in.at[r - 1],
+            square_send.at[r - 1],
+            square_recv.at[r - 1],
+            peers[r],
+        )
+        copy.start()
+        square_copies.append(copy)
+    for copy in square_copies:
+        copy.wait_recv()
+    for r in range(3):
+        squares = squares + square_in[r][:, 0:1]
+    inverse = lax.rsqrt(squares / width + 1e-06)
+    normed = (state * inverse * gain_ref[:, columns]).astype(BF16)
+    own_normed[...] = normed
+    gather = Gather(
+        n_exp, own_normed, lambda index: normed_all.at[index], token_send, token_recv
+    )
+    gather.start()
+    normed_all[me] = normed
+    gather.forward()
+    gather.finish()
+    for copy in copies + square_copies:
+        copy.wait_send()
+
+
+def expert_kernel(
+    n_exp,
+    capacity,
+    normed_ref,
+    cot_ref,
+    meta_ref,
+    state_ref,
+    gate_ref,
+    up_ref,
+    down_ref,
+    layer_ref,
+    grad_gate_ref,
+    grad_up_ref,
+    grad_down_ref,
+    slot_in,
+    slot_grad,
+    picks,
+    slot_prob,
+    core_out,
+    core_in,
+    side_out,
+    side_in,
+    own_sum,
+    acts,
+    scaled,
+    back_out,
+    back_in,
+    core_send,
+    core_recv,
+    side_send,
+    side_recv,
+    act_send,
+    act_recv,
+    back_send,
+    back_recv,
+):
+    ctx, head, exp = lax.axis_index("ctx"), lax.axis_index("head"), lax.axis_index("exp")
+    me = ctx * n_exp + exp
+    blocks, rows, quarter = normed_ref.shape
+    experts, hidden_units = gate_ref.shape[:2]
+    share = blocks * capacity // 4
+    core_peer, side_peer = ring_id(ctx, head ^ 1, exp), ring_id(ctx, head ^ 2, exp)
+    others = token_group(n_exp)
+    greet([core_peer, side_peer] + [device for _, device, _, _ in others])
+
+    def place(e, s):
+        return pl.ds(pl.multiple_of((e * blocks + s) * capacity, 16), capacity)
+
+    for e in range(experts):
+
+        @pl.loop(0, blocks)
+        def _(s):
+            meta = meta_ref[s]
+            weight, rank = meta[e : e + 1, :], meta[4 + e : 5 + e, :]
+            slot = lax.broadcasted_iota(jnp.int32, (capacity, rows), 0).astype(F32)
+            pick = jnp.where((slot == rank) & (weight > 0.0), 1.0, 0.0)
+            prob = jnp.sum(pick * weight, axis=1, keepdims=True)
+            pick = pick.astype(BF16)
+            picks[e * blocks + s] = pick
+            slot_prob[place(e, s), :] = jnp.broadcast_to(prob, (capacity, 128))
+            slot_in[place(e, s), :] = jnp.dot(
+                pick, normed_ref[s], preferred_element_type=F32
+            ).astype(BF16)
+            slot_grad[place(e, s), :] = (
+                prob * jnp.dot(pick, cot_ref[s], preferred_element_type=F32)
+            ).astype(BF16)
+
+    kinds = ((slot_in, gate_ref), (slot_in, up_ref), (slot_grad, down_ref))
+    sent = []
+
+    def rows_of(e, index):
+        return pl.ds(pl.multiple_of(e * 4 * share + index * share, 16), share)
+
+    def own_rows(index):
+        return pl.ds(pl.multiple_of(index * share, 16), share)
+
+    def partial(kind, e, index):
+        data, weight = kinds[kind]
+        return lax.dot_general(
+            data[rows_of(e, index), :],
+            weight[e],
+            (((1,), (1,)), ((), ())),
+            preferred_element_type=F32,
+        )
+
+    def begin(copy):
+        copy.start()
+        sent.append(copy)
+
+    def core_copy(kind, e):
+        n = kind * experts + e
+        return remote(
+            core_out.at[n], core_in.at[n], core_send.at[n], core_recv.at[n], core_peer
+        )
+
+    def side_copy(kind, e):
+        n = kind * experts + e
+        return remote(
+            side_out.at[n], side_in.at[n], side_send.at[n], side_recv.at[n], side_peer
+        )
+
+    def reduce_start(kind, e):
+        n = kind * experts + e
+        core_out[n, 1] = partial(kind, e, head ^ 3).astype(BF16)
+        core_out[n, 0] = partial(kind, e, head ^ 1).astype(BF16)
+        begin(core_copy(kind, e))
+        crossing = partial(kind, e, head ^ 2)
+        core_copy(kind, e).wait_recv()
+        side_out[n] = (crossing + core_in[n, 1].astype(F32)).astype(BF16)
+        begin(side_copy(kind, e))
+        own_sum[n] = partial(kind, e, head) + core_in[n, 0].astype(F32)
+
+    def reduced(kind, e):
+        n = kind * experts + e
+        side_copy(kind, e).wait_recv()
+        return own_sum[n] + side_in[n].astype(F32)
+
+    def act_copy(kind, e, index, way):
+        n = kind * experts + e
+        view = acts.at[n, own_rows(index), :]
+        device = side_peer if way == 0 else core_peer
+        return remote(view, view, act_send.at[n * 3 + way], act_recv.at[n * 3 + way], device)
+
+    def spread(kind, e, value):
+        acts[kind * experts + e, own_rows(head), :] = value
+        begin(act_copy(kind, e, head, 0))
+        begin(act_copy(kind, e, head, 1))
+
+    def pass_on(kind, e):
+        act_copy(kind, e, head ^ 2, 0).wait_recv()
+        begin(act_copy(kind, e, head ^ 2, 2))
+
+    def spread_done(kind, e):
+        act_copy(kind, e, head ^ 1, 1).wait_recv()
+        act_copy(kind, e, head ^ 3, 2).wait_recv()
+
+    for e in range(experts):
+        for kind in (0, 1):
+            reduce_start(kind, e)
+    for e in range(experts):
+        gate, up = reduced(0, e), reduced(1, e)
+        own_sum[e], own_sum[experts + e] = gate, up
+        sigma = 1.0 / (1.0 + jnp.exp(-gate))
+        spread(0, e, (gate * sigma * up).astype(BF16))
+        reduce_start(2, e)
+
+    def weight_grad(kind, e, out, data):
+        n = kind * experts + e
+        source = data[pl.ds(e * 4 * share, 4 * share), :]
+        for first in range(0, hidden_units, 256):
+            out[e, first : first + 256, :] = lax.dot_general(
+                acts[n, :, first : first + 256],
+                source,
+                (((0,), (0,)), ((), ())),
+                preferred_element_type=F32,
+            ).astype(BF16)
+
+    for e in range(experts):
+        pass_on(0, e)
+    for e in range(experts):
+        grad = reduced(2, e)
+        gate, up = own_sum[e], own_sum[experts + e]
+        sigma = 1.0 / (1.0 + jnp.exp(-gate))
+        spread(1, e, (grad * up * sigma * (1.0 + gate * (1.0 - sigma))).astype(BF16))
+        spread(2, e, (grad * gate * sigma).astype(BF16))
+    for e in range(experts):
+        spread_done(0, e)
+        for index in range(4):
+            part = pl.ds(index * share, share)
+            whole = pl.ds((e * 4 + index) * share, share)
+            out = jnp.dot(acts[e, part, :], down_ref[e], preferred_element_type=F32)
+            out = out.astype(BF16).astype(F32)
+            scaled[whole, :] = (slot_prob[whole, 0:1] * out).astype(BF16)
+
+    @pl.loop(0, blocks)
+    def _(s):
+        total = jnp.zeros((rows, quarter), F32)
+        for e in range(experts):
+            total = total + lax.dot_general(
+                picks[e * blocks + s],
+                scaled[place(e, s), :],
+                (((0,), (0,)), ((), ())),
+                preferred_element_type=F32,
+            )
+        back_out[s] = total.astype(BF16)
+
+    for sem, device, to_block, _ in others:
+        begin(
+            remote(
+                back_out.at[to_block],
+                back_in.at[sem],
+                back_send.at[sem],
+                back_recv.at[sem],
+                device,
+            )
+        )
+    for e in range(experts):
+        weight_grad(0, e, grad_down_ref, slot_grad)
+    for e in range(experts):
+        for kind, out in ((1, grad_gate_ref), (2, grad_up_ref)):
+            pass_on(kind, e)
+            spread_done(kind, e)
+            weight_grad(kind, e, out, slot_in)
+    total = state_ref[...].astype(F32) + back_out[me].astype(F32)
+    for sem, device, to_block, _ in others:
+        remote(
+            back_out.at[to_block], back_in.at[sem], back_send.at[sem], back_recv.at[sem], device
+        ).wait_recv()
+        total = total + back_in[sem].astype(F32)
+    layer_ref[...] = total.astype(BF16)
+    for copy in sent:
+        copy.wait_send()
+
+
+def per_device(
+    resid,
+    queries,
+    rotated_key_value_pairs,
+    doc_ids,
+    out_weight,
+    norm_gain,
+    routes,
+    probs,
+    w_gate,
+    w_up,
+    w_down,
+    cotangent,
+):
+    rows, width = resid.shape
+    n_ctx, n_exp, n_head = (lax.axis_size(name) for name in ("ctx", "exp", "head"))
+    experts_here, hidden_units, quarter = w_gate.shape
+    owners = n_ctx * n_exp
+    experts = experts_here * owners
+    capacity = rows * routes.shape[1] * 5 // (4 * experts)
+    if (
+        n_ctx != 2
+        or n_head != 4
+        or experts_here != 2
+        or capacity % 16
+        or capacity * experts_here < rows
+        or rotated_key_value_pairs.shape[2] != HEAD_DIMENSION
+    ):
+        return per_device_slots(
+            resid,
+            queries,
+            rotated_key_value_pairs,
+            doc_ids,
+            out_weight,
+            norm_gain,
+            routes,
+            probs,
+            w_gate,
+            w_up,
+            w_down,
+            cotangent,
+        )
+    dma = pltpu.SemaphoreType.DMA
+    vmem = pl.BlockSpec(memory_space=pltpu.VMEM)
+    shape = jax.ShapeDtypeStruct
+
+    def params(number, mib):
+        return pltpu.CompilerParams(
+            collective_id=number, has_side_effects=True, vmem_limit_bytes=mib << 20
+        )
+
+    full_weight = lax.all_gather(out_weight, ("ctx", "exp"), axis=1, tiled=True)
+    named = routes[:, :, None] == jnp.arange(experts, dtype=jnp.int32)[None, None, :]
+    share = jnp.sum(jnp.where(named, probs[:, :, None], 0.0), axis=1)
+    mask = jnp.any(named, axis=1).astype(BF16)
+    earlier = jnp.tril(jnp.ones((rows, rows), BF16), -1)
+    rank = jnp.dot(earlier, mask, preferred_element_type=F32)
+    doc = doc_ids.astype(F32)
+    spare = jnp.zeros((owners, 2, rows), F32)
+    meta = jnp.concatenate(
+        [
+            share.T.reshape(owners, 2, rows),
+            jnp.broadcast_to(doc[None], (owners, 2, rows)),
+            rank.T.reshape(owners, 2, rows),
+            spare,
+        ],
+        axis=1,
+    )
+    doc_column = jnp.broadcast_to(doc.T, (rows, 128))
+    heads = queries.shape[1] // HEAD_DIMENSION
+    total = owners * rows
+    attn, cot_all, meta_all = pl.pallas_call(
+        functools.partial(attention_kernel, n_exp, heads),
+        out_shape=(
+            shape(queries.shape, BF16),
+            shape((owners, rows, quarter), BF16),
+            shape(meta.shape, F32),
+        ),
+        in_specs=[vmem] * 5,
+        out_specs=(vmem,) * 3,
+        scratch_shapes=[
+            pltpu.VMEM((2, total, HEAD_DIMENSION), BF16),
+            dma((owners,)),
+            dma((owners,)),
+        ]
+        + [dma((2 * n_exp,))] * 4,
+        compiler_params=params(1, 24),
+    )(rotated_key_value_pairs, queries, doc_column, meta, cotangent)
+    state, normed_all = pl.pallas_call(
+        functools.partial(norm_kernel, n_exp),
+        out_shape=(shape((rows, quarter), BF16), shape((owners, rows, quarter), BF16)),
+        in_specs=[vmem] * 4,
+        out_specs=(vmem,) * 2,
+        scratch_shapes=[
+            pltpu.VMEM((3, rows, quarter), BF16),
+            pltpu.VMEM((3, rows, quarter), BF16),
+            pltpu.VMEM((rows, 128), F32),
+            pltpu.VMEM((3, rows, 128), F32),
+            pltpu.VMEM((rows, quarter), BF16),
+        ]
+        + [dma((3,))] * 4
+        + [dma((2 * n_exp,))] * 2,
+        compiler_params=params(2, 24),
+    )(attn, full_weight, resid, norm_gain.reshape(1, width))
+    slots = experts_here * owners * capacity
+    quarter_rows = owners * capacity // 4
+    pairs = 3 * experts_here
+    grad_shape = shape(w_gate.shape, BF16)
+    return pl.pallas_call(
+        functools.partial(expert_kernel, n_exp, capacity),
+        out_shape=(shape((rows, quarter), BF16), grad_shape, grad_shape, grad_shape),
+        in_specs=[vmem] * 7,
+        out_specs=(vmem,) * 4,
+        scratch_shapes=[
+            pltpu.VMEM((slots, quarter), BF16),
+            pltpu.VMEM((slots, quarter), BF16),
+            pltpu.VMEM((experts_here * owners, capacity, rows), BF16),
+            pltpu.VMEM((slots, 128), F32),
+            pltpu.VMEM((pairs, 2, quarter_rows, hidden_units), BF16),
+            pltpu.VMEM((pairs, 2, quarter_rows, hidden_units), BF16),
+            pltpu.VMEM((pairs, quarter_rows, hidden_units), BF16),
+            pltpu.VMEM((pairs, quarter_rows, hidden_units), BF16),
+            pltpu.VMEM((pairs, quarter_rows, hidden_units), F32),
+            pltpu.VMEM((pairs, 4 * quarter_rows, hidden_units), BF16),
+            pltpu.VMEM((slots, quarter), BF16),
+            pltpu.VMEM((owners, rows, quarter), BF16),
+            pltpu.VMEM((owners, rows, quarter), BF16),
+        ]
+        + [dma((pairs,))] * 4
+        + [dma((3 * pairs,))] * 2
+        + [dma((owners,))] * 2,
+        compiler_params=params(3, 56),
+    )(normed_all, cot_all, meta_all, state, w_gate, w_up, w_down)
+
+
 def solution(mesh):
     return jax.shard_map(
         per_device,

time: 441 us -> 237 us (0.54)
  Pallas kernels: 0 us -> 163 us
  waiting for transfers between devices: 158 us -> 41.5 us
  blocking collectives: 95.3 us -> 0 us
  local copies, waits for them, and re-layouts: 98.8 us -> 15.9 us
  matrix products: 40.1 us -> 0.2 us
  starting transfers between devices: 15.9 us -> 0.04 us
  other arithmetic: 15.2 us -> 2.17 us
    pallas_call x0 -> x3, Pallas kernels: none -> 163 us  [the longest x1 89.1 us: per_device(): pl.pallas_call(functools.partial(expert_kernel, n_exp, capacity), out_sha...]
    unnamed x11 -> x1, waiting for transfers between devices: 64.4 us -> 0.68 us
    all_to_all x2 -> x0, blocking collectives: 50.4 us -> none  [the longest x1 32.7 us: per_device(): lax.all_to_all(lax.all_to_all(send_rows.reshape(n_ctx, n_exp, exp_dev * c...]
    all_gather x2 -> x0, blocking collectives: 44.9 us -> none  [the longest x1 31.2 us: per_device(): lax.all_gather(rotated_key_value_pairs, ('ctx', 'exp'), axis=1, tiled=True)]
    unnamed x39 -> x28, local copies, waits for them, and re-layouts: 58.2 us -> 15.7 us
    dot_general x10 -> x1, matrix products: 34.1 us -> 0.2 us  [per_device(): rank = jnp.dot(earlier, mask, preferred_element_type=F32)]
    all_gather x4 -> x1, waiting for transfers between devices: 65.8 us -> 40.8 us  [per_device(): full_weight = lax.all_gather(out_weight, ('ctx', 'exp'), axis=1, tiled=True)]
    psum x1 -> x0, waiting for transfers between devices: 23.5 us -> none  [per_device(): attn_sum = lax.psum(partial_value, 'head')]
  transfers between devices with their start and end apart: 11 -> 1, of which waited for: 7 -> 1; matrix products, arithmetic and copies ran while one was open for 30% -> 1% of each run, Pallas kernels for 0% -> 17%
where the time goes in v1:
time: 237 us
  Pallas kernels  163 us (69%)
  waiting for transfers between devices  41.5 us (18%)
  local copies, waits for them, and re-layouts  15.9 us (7%)
  between operations  14.1 us (6%)
    pallas_call x1, Pallas kernels, per_device(): pl.pallas_call(functools.partial(expert_kernel, n_exp, capacity), out_sha...  89.1 us
    all_gather x1, waiting for transfers between devices, per_device(): full_weight = lax.all_gather(out_weight, ('ctx', 'exp'), axis=1, tiled=True)  40.8 us
    pallas_call x1, Pallas kernels, per_device(): pl.pallas_call(functools.partial(attention_kernel, n_exp, heads), out_sha...  40.8 us
    pallas_call x1, Pallas kernels, per_device(): pl.pallas_call(functools.partial(norm_kernel, n_exp), out_shape=(shape((r...  33.1 us
    unnamed x28, local copies, waits for them, and re-layouts  15.7 us
  transfers between devices with their start and end apart: 1, of which 1 were waited for; matrix products, arithmetic and copies ran while one was open for 1% of the time, Pallas kernels for 17%

profile of v1, /device:TPU:9, one launch (start us, length us, event | category | flops | bytes accessed | tf_op | source)
XLA Modules:
  0.0 237.0 jit_solution(8815365501092660575)
XLA Ops:
  7.2 0.0 copy-start.9
  7.2 0.0 copy-start.3
  7.2 0.0 all-gather.2.cloned.1.call-start
  7.2 0.7 all-gather.2.cloned.1.call-update
  7.9 0.7 fusion
  8.6 0.2 fusion.3
  8.9 0.1 pad.3.clone
  8.9 0.7 select_reduce_fusion
  9.7 0.7 convert_bitcast_fusion
  10.3 0.1 maximum_maximum_fusion.meta_ref
  10.4 0.1 broadcast_in_dim.39.doc_ref
  10.5 1.0 copy-done.4
  11.5 0.9 copy-done.5
  12.5 0.8 copy-done.7
  13.3 40.8 %shard_map.147 = (bf16[128,1024]{1,0:T(8,128)(2,1)S(1)}, bf16[8,128,512]{2,1,0:T(8,128)(2,1)S(1)}, f32[8,8,128]{2,1,0:T(8,128)S(1)}) custom-call(bf16[2,128,128]{2,1,0:T(8,128)(2,1)S(1)} %copy-done.7, bf16[128,1024]{1,0:T(8,128)(2,1)S(1)} %copy-done.5, f32[128,128]{1,0:T(8,128)S(1)} %broadcast_in_dim.39.doc_ref, ...), custom_call_target="tpu_custom_call" | custom-call | tf_op jit(solution)/shard_map/pallas_call | solution.py:747
  54.2 0.0 copy-start.1
  54.2 1.0 copy-done.1
  55.2 0.6 copy-done.8
  55.8 40.8 %all-gather.2.cloned.1.call-done.weight_ref = bf16[1024,2048]{1,0:T(8,128)(2,1)} async-done(((bf16[1024,256]{1,0:T(8,128)(2,1)}), bf16[1024,2048]{1,0:T(8,128)(2,1)}) %all-gather.2.cloned.1.call-update) | async-done | bytes 4194320 | tf_op jit(solution)/shard_map/all_gather | solution.py:727
  96.6 0.0 copy-done.9
  96.6 0.0 copy-done.3
  96.6 2.2 copy-done
  98.8 33.1 %shard_map.148 = (bf16[128,512]{1,0:T(8,128)(2,1)S(1)}, bf16[8,128,512]{2,1,0:T(8,128)(2,1)S(1)}) custom-call(bf16[128,1024]{1,0:T(8,128)(2,1)S(1)} %get-tuple-element.9.attn_ref, bf16[1024,2048]{1,0:T(8,128)(2,1)S(1)} %copy-done, bf16[128,2048]{1,0:T(8,128)(2,1)S(1)} %copy-done.3, f32[1,2048]{1,0:T(1,128)S(1)} %bitcast.10), custom_call_target="tpu_custom_call" | custom-call | tf_op jit(solution)/shard_map/pallas_call | solution.py:764
  131.9 0.0 copy-start.2
  131.9 1.0 copy-done.2
  132.9 0.7 copy-done.6
  133.5 89.1 %shard_map.149 = (bf16[128,512]{1,0:T(8,128)(2,1)}, bf16[2,768,512]{2,1,0:T(8,128)(2,1)}, bf16[2,768,512]{2,1,0:T(8,128)(2,1)}, bf16[2,768,512]{2,1,0:T(8,128)(2,1)}) custom-call(bf16[8,128,512]{2,1,0:T(8,128)(2,1)} %copy-done.2, bf16[8,128,512]{2,1,0:T(8,128)(2,1)} %copy-done.1, f32[8,8,128]{2,1,0:T(8,128)} %copy-done.8, bf16[128,512]{1,0:T(8,128)(2,1)} %copy-done.6, ...), custom_call_target="tpu_custom_call" | custom-call | tf_op jit(solution)/shard_map/pallas_call | solution.py:784
  222.7 1.6 copy.31
  224.3 2.8 %copy.32 = bf16[2,768,512]{2,1,0:T(8,128)(2,1)} copy(bf16[2,768,512]{2,1,0:T(8,128)(2,1)} %get-tuple-element.19) | data formatting | bytes 3145728
  227.0 1.1 copy.33
  228.2 0.8 copy-done.10
  229.0 1.1 copy.34
  (14 shorter events, 0.0 us)
Async XLA Ops:
  7.2 89.5 %copy-start.9 = (f32[2048]{0:T(1024)S(1)}, f32[2048]{0:T(1024)}, u32[]{:S(2)}) copy-start(f32[2048]{0:T(1024)} %param.17) | copy-start | bytes 24580
  7.2 89.4 %copy-start.3 = (bf16[128,2048]{1,0:T(8,128)(2,1)S(1)}, bf16[128,2048]{1,0:T(8,128)(2,1)}, u32[]{:S(2)}) copy-start(bf16[128,2048]{1,0:T(8,128)(2,1)} %resid_ref.1) | copy-start | bytes 1572868
  7.2 89.4 %all-gather.2.cloned.1.call-start = ((), (), s32[]{:S(2)}) async-start(), calls=%async_computation | async-start | bytes 4718592 | tf_op jit(solution)/shard_map/all_gather | solution.py:727
  10.5 1.1 copy-start.4
  11.5 0.9 copy-start.5
  12.5 0.8 copy-start.7
  54.2 1.0 copy-start.1
  55.2 0.6 copy-start.8
  96.6 2.2 copy-start
  131.9 1.0 copy-start.2
  132.9 0.7 copy-start.6
  224.3 2.8 %copy-start.11 = (bf16[2,768,512]{2,1,0:T(8,128)(2,1)S(1)}, bf16[2,768,512]{2,1,0:T(8,128)(2,1)}, u32[]{:S(2)}) copy-start(bf16[2,768,512]{2,1,0:T(8,128)(2,1)} %get-tuple-element.20) | copy-start | bytes 4718596
  227.0 2.0 copy-start.10
Sparse Core Ops, SparseCore 0:
  10.0 86.5 all-gather.1

commit v2 on v1

--- a/solution.py
+++ b/solution.py
@@ -294,178 +294,19 @@
             self.arrived(
                 other + lax.rem(self.exp + self.n_exp - dz, self.n_exp), self.n_exp + dz
             )
-        for copy in self.sent:
-            copy.wait_send()
-
-
-def attention_kernel(
+
+
+def layer_kernel(
     n_exp,
-    heads,
+    capacity,
     kv_ref,
     query_ref,
     doc_ref,
     meta_ref,
     cot_ref,
-    attn_ref,
-    cot_all,
-    meta_all,
-    kv_all,
-    meta_send,
-    meta_recv,
-    kv_send,
-    kv_recv,
-    cot_send,
-    cot_recv,
-):
-    rows, quarter = cot_all.shape[1:]
-    me = lax.axis_index("ctx") * n_exp + lax.axis_index("exp")
-    others = token_group(n_exp)
-    greet([device for _, device, _, _ in others])
-
-    def kv_block(index):
-        return kv_all.at[:, pl.ds(pl.multiple_of(index * rows, rows), rows), :]
-
-    kv_gather = Gather(n_exp, kv_ref, kv_block, kv_send, kv_recv)
-    kv_gather.start()
-    meta_copies = []
-    for sem, device, to_block, _ in others:
-        copy = remote(
-            meta_ref.at[to_block], meta_all.at[me], meta_send.at[sem], meta_recv.at[sem], device
-        )
-        copy.start()
-        meta_copies.append(copy)
-    kv_all[:, pl.ds(pl.multiple_of(me * rows, rows), rows), :] = kv_ref[...]
-    meta_all[me] = meta_ref[me]
-    column = pl.multiple_of(lax.axis_index("head") * quarter, quarter)
-    own_cot = cot_ref.at[:, pl.ds(column, quarter)]
-    kv_gather.forward()
-    cot_gather = Gather(n_exp, own_cot, lambda index: cot_all.at[index], cot_send, cot_recv)
-    cot_gather.start()
-    cot_all[me] = cot_ref[:, pl.ds(column, quarter)]
-    kv_gather.finish()
-    for sem, device, _, from_block in others:
-        remote(
-            meta_all.at[from_block],
-            meta_all.at[from_block],
-            meta_send.at[sem],
-            meta_recv.at[sem],
-            device,
-        ).wait_recv()
-    for copy in meta_copies:
-        copy.wait_send()
-
-    total = kv_all.shape[1]
-    key_doc = jnp.concatenate([meta_all[s, 2:3, :] for s in range(total // rows)], axis=1)
-    key_pos = lax.broadcasted_iota(jnp.int32, (rows, total), 1)
-    query_pos = me * rows + lax.broadcasted_iota(jnp.int32, (rows, total), 0)
-    visible = (key_pos <= query_pos) & (key_doc == doc_ref[:, 0:1])
-    scale = HEAD_DIMENSION ** (-0.5)
-    for head in range(heads):
-        lanes = slice(head * HEAD_DIMENSION, (head + 1) * HEAD_DIMENSION)
-        scores = lax.dot_general(
-            query_ref[:, lanes], kv_all[0], (((1,), (1,)), ((), ())), preferred_element_type=F32
-        )
-        scores = jnp.where(visible, scores * scale, -1e30)
-        weights = jnp.exp(scores - jnp.max(scores, axis=1, keepdims=True))
-        row_total = jnp.sum(weights, axis=1, keepdims=True)
-        mixed = jnp.dot(weights.astype(BF16), kv_all[1], preferred_element_type=F32)
-        attn_ref[:, lanes] = (mixed / row_total).astype(BF16)
-        if head == heads // 2:
-            cot_gather.forward()
-    cot_gather.finish()
-
-
-def norm_kernel(
-    n_exp,
-    attn_ref,
     weight_ref,
     resid_ref,
     gain_ref,
-    state_ref,
-    normed_all,
-    part_out,
-    part_in,
-    square_out,
-    square_in,
-    own_normed,
-    part_send,
-    part_recv,
-    square_send,
-    square_recv,
-    token_send,
-    token_recv,
-):
-    ctx, head, exp = lax.axis_index("ctx"), lax.axis_index("head"), lax.axis_index("exp")
-    me = ctx * n_exp + exp
-    rows, quarter = state_ref.shape
-    width = resid_ref.shape[1]
-    peers = {r: ring_id(ctx, head ^ r, exp) for r in (1, 2, 3)}
-    along = [ring_id(ctx, head, lax.rem(exp + dz, n_exp)) for dz in range(1, n_exp)]
-    greet([peers[r] for r in (1, 2, 3)] + along + [ring_id(1 - ctx, head, exp)])
-
-    def partial(index):
-        columns = pl.ds(pl.multiple_of(index * quarter, quarter), quarter)
-        return jnp.dot(attn_ref[...], weight_ref[:, columns], preferred_element_type=F32)
-
-    copies = []
-    for r in (2, 3, 1):
-        part_out[r - 1] = partial(head ^ r).astype(BF16)
-        copy = remote(
-            part_out.at[r - 1],
-            part_in.at[r - 1],
-            part_send.at[r - 1],
-            part_recv.at[r - 1],
-            peers[r],
-        )
-        copy.start()
-        copies.append(copy)
-    columns = pl.ds(pl.multiple_of(head * quarter, quarter), quarter)
-    state = partial(head)
-    for copy in copies:
-        copy.wait_recv()
-    for r in range(3):
-        state = state + part_in[r].astype(F32)
-    state = (resid_ref[:, columns].astype(F32) + state).astype(BF16)
-    state_ref[...] = state
-    state = state.astype(F32)
-    squares = jnp.sum(state * state, axis=1, keepdims=True)
-    square_out[...] = jnp.broadcast_to(squares, square_out.shape)
-    square_copies = []
-    for r in (2, 3, 1):
-        copy = remote(
-            square_out,
-            square_in.at[r - 1],
-            square_send.at[r - 1],
-            square_recv.at[r - 1],
-            peers[r],
-        )
-        copy.start()
-        square_copies.append(copy)
-    for copy in square_copies:
-        copy.wait_recv()
-    for r in range(3):
-        squares = squares + square_in[r][:, 0:1]
-    inverse = lax.rsqrt(squares / width + 1e-06)
-    normed = (state * inverse * gain_ref[:, columns]).astype(BF16)
-    own_normed[...] = normed
-    gather = Gather(
-        n_exp, own_normed, lambda index: normed_all.at[index], token_send, token_recv
-    )
-    gather.start()
-    normed_all[me] = normed
-    gather.forward()
-    gather.finish()
-    for copy in copies + square_copies:
-        copy.wait_send()
-
-
-def expert_kernel(
-    n_exp,
-    capacity,
-    normed_ref,
-    cot_ref,
-    meta_ref,
-    state_ref,
     gate_ref,
     up_ref,
     down_ref,
@@ -473,6 +314,19 @@
     grad_gate_ref,
     grad_up_ref,
     grad_down_ref,
+    kv_all,
+    cot_all,
+    meta_all,
+    weight_all,
+    attn_all,
+    part_out,
+    part_in,
+    cols_out,
+    cols_in,
+    square_out,
+    square_in,
+    own_normed,
+    normed_all,
     slot_in,
     slot_grad,
     picks,
@@ -486,6 +340,24 @@
     scaled,
     back_out,
     back_in,
+    meta_send,
+    meta_recv,
+    kv_send,
+    kv_recv,
+    cot_send,
+    cot_recv,
+    weight_send,
+    weight_recv,
+    line_send,
+    line_recv,
+    part_send,
+    part_recv,
+    cols_send,
+    cols_recv,
+    square_send,
+    square_recv,
+    token_send,
+    token_recv,
     core_send,
     core_recv,
     side_send,
@@ -497,21 +369,137 @@
 ):
     ctx, head, exp = lax.axis_index("ctx"), lax.axis_index("head"), lax.axis_index("exp")
     me = ctx * n_exp + exp
-    blocks, rows, quarter = normed_ref.shape
+    blocks, rows, quarter = normed_all.shape
+    width = resid_ref.shape[1]
     experts, hidden_units = gate_ref.shape[:2]
     share = blocks * capacity // 4
+    half = quarter // 2
     core_peer, side_peer = ring_id(ctx, head ^ 1, exp), ring_id(ctx, head ^ 2, exp)
+    across = ring_id(1 - ctx, head, exp)
     others = token_group(n_exp)
-    greet([core_peer, side_peer] + [device for _, device, _, _ in others])
+    greet(
+        [
+            ring_id(ctx, head ^ r, lax.rem(exp + dz, n_exp))
+            for r in range(4)
+            for dz in range(n_exp)
+            if r or dz
+        ]
+        + [ring_id(1 - ctx, head, lax.rem(exp + dz, n_exp)) for dz in range(n_exp)]
+    )
+    sent = []
+
+    def begin(copy):
+        copy.start()
+        sent.append(copy)
+
+    def kv_block(index):
+        return kv_all.at[:, pl.ds(pl.multiple_of(index * rows, rows), rows), :]
+
+    kv_gather = Gather(n_exp, kv_ref, kv_block, kv_send, kv_recv)
+    kv_gather.start()
+    for sem, device, to_block, _ in others:
+        begin(
+            remote(
+                meta_ref.at[to_block], meta_all.at[me], meta_send.at[sem], meta_recv.at[sem], device
+            )
+        )
+    kv_all[:, pl.ds(pl.multiple_of(me * rows, rows), rows), :] = kv_ref[...]
+    meta_all[me] = meta_ref[me]
+    kv_gather.forward()
+    begin(
+        remote(weight_ref, weight_all.at[ctx], weight_send.at[0], weight_recv.at[0], across)
+    )
+    weight_all[ctx] = weight_ref[...]
+    columns = pl.ds(pl.multiple_of(head * quarter, quarter), quarter)
+    cot_gather = Gather(
+        n_exp, cot_ref.at[:, columns], lambda index: cot_all.at[index], cot_send, cot_recv
+    )
+    cot_gather.start()
+    cot_all[me] = cot_ref[:, columns]
+    for sem, device, _, from_block in others:
+        remote(
+            meta_all.at[from_block],
+            meta_all.at[from_block],
+            meta_send.at[sem],
+            meta_recv.at[sem],
+            device,
+        ).wait_recv()
+    kv_gather.finish()
+
+    total = kv_all.shape[1]
+    key_doc = jnp.concatenate([meta_all[s, 2:3, :] for s in range(total // rows)], axis=1)
+    key_pos = lax.broadcasted_iota(jnp.int32, (rows, total), 1)
+    query_pos = me * rows + lax.broadcasted_iota(jnp.int32, (rows, total), 0)
+    visible = (key_pos <= query_pos) & (key_doc == doc_ref[:, 0:1])
+    scale = HEAD_DIMENSION ** (-0.5)
+    heads = query_ref.shape[1] // HEAD_DIMENSION
+    chunks = 4
+    chunk_lanes = query_ref.shape[1] // chunks
+
+    def line_copy(way, c, k, receive):
+        index = exp - k if way == 0 else exp + k
+        view = attn_all.at[index, :, c * chunk_lanes : (c + 1) * chunk_lanes]
+        first = (way * chunks + c) * n_exp
+        device = ring_id(ctx, head, exp + 1 if way == 0 else exp - 1)
+        if receive:
+            device = across
+        return remote(
+            view,
+            view,
+            line_send.at[first + k],
+            line_recv.at[first + (k if receive else k + 1)],
+            device,
+        )
+
+    def holds(way, k):
+        return exp >= k if way == 0 else exp <= n_exp - 1 - k
+
+    def passes(way, k):
+        return holds(way, k) & (exp < n_exp - 1 if way == 0 else exp > 0)
+
+    def line_pass(c, k):
+        for way in range(2):
+            if k:
+
+                @pl.when(holds(way, k))
+                def _():
+                    line_copy(way, c, k, True).wait_recv()
+
+            if k < n_exp - 1:
+
+                @pl.when(passes(way, k))
+                def _():
+                    line_copy(way, c, k, False).start()
+
+    for c in range(chunks):
+        for number in range(c * heads // chunks, (c + 1) * heads // chunks):
+            lanes = slice(number * HEAD_DIMENSION, (number + 1) * HEAD_DIMENSION)
+            scores = lax.dot_general(
+                query_ref[:, lanes], kv_all[0], (((1,), (1,)), ((), ())), preferred_element_type=F32
+            )
+            scores = jnp.where(visible, scores * scale, -1e30)
+            weights = jnp.exp(scores - jnp.max(scores, axis=1, keepdims=True))
+            row_total = jnp.sum(weights, axis=1, keepdims=True)
+            mixed = jnp.dot(weights.astype(BF16), kv_all[1], preferred_element_type=F32)
+            attn_all[exp, :, lanes] = (mixed / row_total).astype(BF16)
+        line_pass(c, 0)
+        if c:
+            line_pass(c - 1, 1)
+        if c == 2:
+            cot_gather.forward()
+    line_pass(chunks - 1, 1)
+    for c in range(chunks):
+        line_pass(c, 2)
 
     def place(e, s):
         return pl.ds(pl.multiple_of((e * blocks + s) * capacity, 16), capacity)
 
+    cot_gather.finish()
     for e in range(experts):
 
         @pl.loop(0, blocks)
         def _(s):
-            meta = meta_ref[s]
+            meta = meta_all[s]
             weight, rank = meta[e : e + 1, :], meta[4 + e : 5 + e, :]
             slot = lax.broadcasted_iota(jnp.int32, (capacity, rows), 0).astype(F32)
             pick = jnp.where((slot == rank) & (weight > 0.0), 1.0, 0.0)
@@ -519,16 +507,107 @@
             pick = pick.astype(BF16)
             picks[e * blocks + s] = pick
             slot_prob[place(e, s), :] = jnp.broadcast_to(prob, (capacity, 128))
-            slot_in[place(e, s), :] = jnp.dot(
-                pick, normed_ref[s], preferred_element_type=F32
+            slot_grad[place(e, s), :] = (
+                prob * jnp.dot(pick, cot_all[s], preferred_element_type=F32)
             ).astype(BF16)
-            slot_grad[place(e, s), :] = (
-                prob * jnp.dot(pick, cot_ref[s], preferred_element_type=F32)
-            ).astype(BF16)
+
+    for c in range(chunks):
+        line_pass(c, 3)
+    weight_view = weight_all.at[1 - ctx]
+    remote(
+        weight_view, weight_view, weight_send.at[0], weight_recv.at[0], across
+    ).wait_recv()
+
+    def projected(index):
+        block = attn_all[index]
+        return jnp.concatenate(
+            [jnp.dot(block, weight_all[p], preferred_element_type=F32) for p in range(2)], axis=1
+        )
+
+    part_copies = []
+    for r in (2, 3, 1):
+        part_out[r - 1] = projected(head ^ r).astype(BF16)
+        copy = remote(
+            part_out.at[r - 1],
+            part_in.at[r - 1],
+            part_send.at[r - 1],
+            part_recv.at[r - 1],
+            ring_id(ctx, head ^ r, exp),
+        )
+        begin(copy)
+        part_copies.append(copy)
+    state = projected(head)
+    for copy in part_copies:
+        copy.wait_recv()
+    for r in range(3):
+        state = state + part_in[r].astype(F32)
+    side = lax.rem(exp, 2)
+    for p in range(2):
+        cols_out[p] = state[:, p * half : (p + 1) * half].astype(BF16)
+
+    def cols_copy(p):
+        target = 2 * p + lax.div(exp, 2)
+        own = (target == head) & (head == exp)
+        copy = remote(
+            cols_out.at[p],
+            cols_in.at[side],
+            cols_send.at[p],
+            cols_recv.at[side],
+            ring_id(ctx, target, head),
+        )
+        return own, copy
+
+    for p in range(2):
+        own, copy = cols_copy(p)
+
+        @pl.when(jnp.logical_not(own))
+        def _():
+            copy.start()
+
+        @pl.when(own)
+        def _():
+            cols_in[side] = cols_out[p]
+
+    for p in range(2):
+        source = 2 * lax.rem(head, 2) + p
+        own = (source == exp) & (head == exp)
+
+        @pl.when(jnp.logical_not(own))
+        def _():
+            view = cols_in.at[p]
+            remote(view, view, cols_send.at[p], cols_recv.at[p], across).wait_recv()
+
+    state = jnp.concatenate([cols_in[0], cols_in[1]], axis=1).astype(F32)
+    state = (resid_ref[:, columns].astype(F32) + state).astype(BF16)
+    layer_ref[...] = state
+    state = state.astype(F32)
+    squares = jnp.sum(state * state, axis=1, keepdims=True)
+    square_out[...] = jnp.broadcast_to(squares, square_out.shape)
+    square_copies = []
+    for r in (2, 3, 1):
+        copy = remote(
+            square_out,
+            square_in.at[r - 1],
+            square_send.at[r - 1],
+            square_recv.at[r - 1],
+            ring_id(ctx, head ^ r, exp),
+        )
+        begin(copy)
+        square_copies.append(copy)
+    for copy in square_copies:
+        copy.wait_recv()
+    for r in range(3):
+        squares = squares + square_in[r][:, 0:1]
+    inverse = lax.rsqrt(squares / width + 1e-06)
+    normed = (state * inverse * gain_ref[:, columns]).astype(BF16)
+    own_normed[...] = normed
+    token_gather = Gather(
+        n_exp, own_normed, lambda index: normed_all.at[index], token_send, token_recv
+    )
+    token_gather.start()
+    normed_all[me] = normed
 
     kinds = ((slot_in, gate_ref), (slot_in, up_ref), (slot_grad, down_ref))
-    sent = []
-
     def rows_of(e, index):
         return pl.ds(pl.multiple_of(e * 4 * share + index * share, 16), share)
 
@@ -543,10 +622,6 @@
             (((1,), (1,)), ((), ())),
             preferred_element_type=F32,
         )
-
-    def begin(copy):
-        copy.start()
-        sent.append(copy)
 
     def core_copy(kind, e):
         n = kind * experts + e
@@ -595,7 +670,19 @@
         act_copy(kind, e, head ^ 1, 1).wait_recv()
         act_copy(kind, e, head ^ 3, 2).wait_recv()
 
+    reduce_start(2, 0)
+    token_gather.forward()
+    for e in range(1, experts):
+        reduce_start(2, e)
+    token_gather.finish()
     for e in range(experts):
+
+        @pl.loop(0, blocks)
+        def _(s):
+            slot_in[place(e, s), :] = jnp.dot(
+                picks[e * blocks + s], normed_all[s], preferred_element_type=F32
+            ).astype(BF16)
+
         for kind in (0, 1):
             reduce_start(kind, e)
     for e in range(experts):
@@ -603,7 +690,6 @@
         own_sum[e], own_sum[experts + e] = gate, up
         sigma = 1.0 / (1.0 + jnp.exp(-gate))
         spread(0, e, (gate * sigma * up).astype(BF16))
-        reduce_start(2, e)
 
     def weight_grad(kind, e, out, data):
         n = kind * experts + e
@@ -662,15 +748,29 @@
             pass_on(kind, e)
             spread_done(kind, e)
             weight_grad(kind, e, out, slot_in)
-    total = state_ref[...].astype(F32) + back_out[me].astype(F32)
+    total = layer_ref[...].astype(F32) + back_out[me].astype(F32)
     for sem, device, to_block, _ in others:
         remote(
             back_out.at[to_block], back_in.at[sem], back_send.at[sem], back_recv.at[sem], device
         ).wait_recv()
         total = total + back_in[sem].astype(F32)
     layer_ref[...] = total.astype(BF16)
-    for copy in sent:
+    for copy in sent + kv_gather.sent + cot_gather.sent + token_gather.sent:
         copy.wait_send()
+    for p in range(2):
+        own, copy = cols_copy(p)
+
+        @pl.when(jnp.logical_not(own))
+        def _():
+            copy.wait_send()
+
+    for way in range(2):
+        for c in range(chunks):
+            for k in range(n_exp - 1):
+
+                @pl.when(passes(way, k))
+                def _():
+                    line_copy(way, c, k, False).wait_send()
 
 
 def per_device(
@@ -696,6 +796,7 @@
     if (
         n_ctx != 2
         or n_head != 4
+        or n_exp != n_head
         or experts_here != 2
         or capacity % 16
         or capacity * experts_here < rows
@@ -719,12 +820,6 @@
     vmem = pl.BlockSpec(memory_space=pltpu.VMEM)
     shape = jax.ShapeDtypeStruct
 
-    def params(number, mib):
-        return pltpu.CompilerParams(
-            collective_id=number, has_side_effects=True, vmem_limit_bytes=mib << 20
-        )
-
-    full_weight = lax.all_gather(out_weight, ("ctx", "exp"), axis=1, tiled=True)
     named = routes[:, :, None] == jnp.arange(experts, dtype=jnp.int32)[None, None, :]
     share = jnp.sum(jnp.where(named, probs[:, :, None], 0.0), axis=1)
     mask = jnp.any(named, axis=1).astype(BF16)
@@ -742,51 +837,31 @@
         axis=1,
     )
     doc_column = jnp.broadcast_to(doc.T, (rows, 128))
-    heads = queries.shape[1] // HEAD_DIMENSION
     total = owners * rows
-    attn, cot_all, meta_all = pl.pallas_call(
-        functools.partial(attention_kernel, n_exp, heads),
-        out_shape=(
-            shape(queries.shape, BF16),
-            shape((owners, rows, quarter), BF16),
-            shape(meta.shape, F32),
-        ),
-        in_specs=[vmem] * 5,
-        out_specs=(vmem,) * 3,
-        scratch_shapes=[
-            pltpu.VMEM((2, total, HEAD_DIMENSION), BF16),
-            dma((owners,)),
-            dma((owners,)),
-        ]
-        + [dma((2 * n_exp,))] * 4,
-        compiler_params=params(1, 24),
-    )(rotated_key_value_pairs, queries, doc_column, meta, cotangent)
-    state, normed_all = pl.pallas_call(
-        functools.partial(norm_kernel, n_exp),
-        out_shape=(shape((rows, quarter), BF16), shape((owners, rows, quarter), BF16)),
-        in_specs=[vmem] * 4,
-        out_specs=(vmem,) * 2,
-        scratch_shapes=[
-            pltpu.VMEM((3, rows, quarter), BF16),
-            pltpu.VMEM((3, rows, quarter), BF16),
-            pltpu.VMEM((rows, 128), F32),
-            pltpu.VMEM((3, rows, 128), F32),
-            pltpu.VMEM((rows, quarter), BF16),
-        ]
-        + [dma((3,))] * 4
-        + [dma((2 * n_exp,))] * 2,
-        compiler_params=params(2, 24),
-    )(attn, full_weight, resid, norm_gain.reshape(1, width))
+    lanes = queries.shape[1]
     slots = experts_here * owners * capacity
     quarter_rows = owners * capacity // 4
     pairs = 3 * experts_here
     grad_shape = shape(w_gate.shape, BF16)
     return pl.pallas_call(
-        functools.partial(expert_kernel, n_exp, capacity),
+        functools.partial(layer_kernel, n_exp, capacity),
         out_shape=(shape((rows, quarter), BF16), grad_shape, grad_shape, grad_shape),
-        in_specs=[vmem] * 7,
+        in_specs=[vmem] * 11,
         out_specs=(vmem,) * 4,
         scratch_shapes=[
+            pltpu.VMEM((2, total, HEAD_DIMENSION), BF16),
+            pltpu.VMEM((owners, rows, quarter), BF16),
+            pltpu.VMEM(meta.shape, F32),
+            pltpu.VMEM((2, lanes, quarter // 2), BF16),
+            pltpu.VMEM((n_exp, rows, lanes), BF16),
+            pltpu.VMEM((3, rows, quarter), BF16),
+            pltpu.VMEM((3, rows, quarter), BF16),
+            pltpu.VMEM((2, rows, quarter // 2), BF16),
+            pltpu.VMEM((2, rows, quarter // 2), BF16),
+            pltpu.VMEM((rows, 128), F32),
+            pltpu.VMEM((3, rows, 128), F32),
+            pltpu.VMEM((rows, quarter), BF16),
+            pltpu.VMEM((owners, rows, quarter), BF16),
             pltpu.VMEM((slots, quarter), BF16),
             pltpu.VMEM((slots, quarter), BF16),
             pltpu.VMEM((experts_here * owners, capacity, rows), BF16),
@@ -800,12 +875,35 @@
             pltpu.VMEM((slots, quarter), BF16),
             pltpu.VMEM((owners, rows, quarter), BF16),
             pltpu.VMEM((owners, rows, quarter), BF16),
+            dma((owners,)),
+            dma((owners,)),
         ]
+        + [dma((2 * n_exp,))] * 4
+        + [dma((1,))] * 2
+        + [dma((8 * n_exp,))] * 2
+        + [dma((3,))] * 2
+        + [dma((2,))] * 2
+        + [dma((3,))] * 2
+        + [dma((2 * n_exp,))] * 2
         + [dma((pairs,))] * 4
         + [dma((3 * pairs,))] * 2
         + [dma((owners,))] * 2,
-        compiler_params=params(3, 56),
-    )(normed_all, cot_all, meta_all, state, w_gate, w_up, w_down)
+        compiler_params=pltpu.CompilerParams(
+            collective_id=1, has_side_effects=True, vmem_limit_bytes=58 << 20
+        ),
+    )(
+        rotated_key_value_pairs,
+        queries,
+        doc_column,
+        meta,
+        cotangent,
+        out_weight,
+        resid,
+        norm_gain.reshape(1, width),
+        w_gate,
+        w_up,
+        w_down,
+    )
 
 
 def solution(mesh):

time: 237 us -> 160 us (0.68)
  waiting for transfers between devices: 41.5 us -> 0 us
  Pallas kernels: 163 us -> 147 us
  between operations: 14.1 us -> 0.66 us
  local copies, waits for them, and re-layouts: 15.9 us -> 8.29 us
    all_gather x1 -> x0, waiting for transfers between devices: 40.8 us -> none  [per_device(): full_weight = lax.all_gather(out_weight, ('ctx', 'exp'), axis=1, tiled=True)]
    pallas_call x3 -> x1, Pallas kernels: 163 us -> 147 us  [per_device(): pl.pallas_call(functools.partial(layer_kernel, n_exp, capacity), out_shap...]
    unnamed x28 -> x8, local copies, waits for them, and re-layouts: 15.7 us -> 7.46 us
  transfers between devices with their start and end apart: 1 -> 0, of which waited for: 1 -> 0; matrix products, arithmetic and copies ran while one was open for 1% -> 0% of each run, Pallas kernels for 17% -> 0%
where the time goes in v2:
time: 160 us; the launch traced here: 159 us
  Pallas kernels  147 us (92%)
  local copies, waits for them, and re-layouts  8.29 us (5%)
  other arithmetic  2.77 us (2%)
    pallas_call x1, Pallas kernels, per_device(): pl.pallas_call(functools.partial(layer_kernel, n_exp, capacity), out_shap...  147 us
    unnamed x8, local copies, waits for them, and re-layouts  7.46 us

profile of v2, /device:TPU:9, one launch (start us, length us, event | category | flops | bytes accessed | tf_op | source)
XLA Modules:
  0.0 159.1 jit_solution(8972768985101708078)
XLA Ops:
  0.6 0.7 convert_bitcast_fusion
  1.3 0.1 pad.3.clone
  1.4 0.7 fusion
  2.1 0.2 fusion.3
  2.3 0.7 select_reduce_fusion
  3.0 0.7 maximum_maximum_fusion.meta_ref
  3.7 0.7 broadcast_in_dim.39.doc_ref
  4.4 147.2 %shard_map.147 = (bf16[128,512]{1,0:T(8,128)(2,1)}, bf16[2,768,512]{2,1,0:T(8,128)(2,1)}, bf16[2,768,512]{2,1,0:T(8,128)(2,1)}, bf16[2,768,512]{2,1,0:T(8,128)(2,1)}) custom-call(bf16[2,128,128]{2,1,0:T(8,128)(2,1)} %kv_ref.1, bf16[128,1024]{1,0:T(8,128)(2,1)} %query_ref.1, f32[128,128]{1,0:T(8,128)} %broadcast_in_dim.39.doc_ref, ...), custom_call_target="tpu_custom_call" | custom-call | tf_op jit(solution)/shard_map/pallas_call | solution.py:846
  151.7 1.6 copy.31
  153.2 0.0 copy-start.1
  153.2 2.8 %copy.32 = bf16[2,768,512]{2,1,0:T(8,128)(2,1)} copy(bf16[2,768,512]{2,1,0:T(8,128)(2,1)} %get-tuple-element.9) | data formatting | bytes 3145728
  156.0 0.0 copy-done.1
  156.0 0.0 copy-start
  156.0 1.1 copy.33
  157.2 0.8 copy-done
  158.0 1.1 copy.34
  (5 shorter events, 0.0 us)
Async XLA Ops:
  153.2 2.8 %copy-start.1 = (bf16[2,768,512]{2,1,0:T(8,128)(2,1)S(1)}, bf16[2,768,512]{2,1,0:T(8,128)(2,1)}, u32[]{:S(2)}) copy-start(bf16[2,768,512]{2,1,0:T(8,128)(2,1)} %get-tuple-element.10) | copy-start | bytes 4718596
  156.0 2.0 %copy-start = (bf16[2,768,512]{2,1,0:T(8,128)(2,1)S(1)}, bf16[2,768,512]{2,1,0:T(8,128)(2,1)}, u32[]{:S(2)}) copy-start(bf16[2,768,512]{2,1,0:T(8,128)(2,1)} %get-tuple-element.11) | copy-start | bytes 4718596

commit v3 on v2

--- a/solution.py
+++ b/solution.py
@@ -302,7 +302,8 @@
     kv_ref,
     query_ref,
     doc_ref,
-    meta_ref,
+    route_ref,
+    prob_ref,
     cot_ref,
     weight_ref,
     resid_ref,
@@ -316,6 +317,7 @@
     grad_down_ref,
     kv_all,
     cot_all,
+    meta_out,
     meta_all,
     weight_all,
     attn_all,
@@ -340,6 +342,7 @@
     scaled,
     back_out,
     back_in,
+    own_back,
     meta_send,
     meta_recv,
     kv_send,
@@ -377,6 +380,24 @@
     core_peer, side_peer = ring_id(ctx, head ^ 1, exp), ring_id(ctx, head ^ 2, exp)
     across = ring_id(1 - ctx, head, exp)
     others = token_group(n_exp)
+    lane = lax.broadcasted_iota(jnp.int32, (rows, 128), 1)
+    weight_of = jnp.zeros((rows, 128), F32)
+    for k in range(route_ref.shape[1]):
+        weight_of = weight_of + jnp.where(
+            route_ref[:, k : k + 1] == lane, prob_ref[:, k : k + 1], 0.0
+        )
+    earlier = jnp.where(lax.broadcasted_iota(jnp.int32, (rows, 128), 0) > lane, 1.0, 0.0)
+    mask = jnp.where(weight_of > 0.0, 1.0, 0.0)
+    rank_of = jnp.dot(earlier.astype(BF16), mask.astype(BF16), preferred_element_type=F32)
+    weight_of, rank_of = weight_of.T, rank_of.T
+    doc_row = doc_ref[...].astype(F32)
+    doc_column = jnp.broadcast_to(doc_row, (rows, 128)).T
+    for owner in range(blocks):
+        mine = slice(owner * experts, (owner + 1) * experts)
+        meta_out[owner, 0:2, :] = weight_of[mine, :]
+        meta_out[owner, 2:4, :] = jnp.broadcast_to(doc_row, (2, rows))
+        meta_out[owner, 4:6, :] = rank_of[mine, :]
+        meta_out[owner, 6:8, :] = jnp.zeros((2, rows), F32)
     greet(
         [
             ring_id(ctx, head ^ r, lax.rem(exp + dz, n_exp))
@@ -396,26 +417,16 @@
         return kv_all.at[:, pl.ds(pl.multiple_of(index * rows, rows), rows), :]
 
     kv_gather = Gather(n_exp, kv_ref, kv_block, kv_send, kv_recv)
-    kv_gather.start()
     for sem, device, to_block, _ in others:
         begin(
             remote(
-                meta_ref.at[to_block], meta_all.at[me], meta_send.at[sem], meta_recv.at[sem], device
+                meta_out.at[to_block], meta_all.at[me], meta_send.at[sem], meta_recv.at[sem], device
             )
         )
+    kv_gather.start()
     kv_all[:, pl.ds(pl.multiple_of(me * rows, rows), rows), :] = kv_ref[...]
-    meta_all[me] = meta_ref[me]
-    kv_gather.forward()
-    begin(
-        remote(weight_ref, weight_all.at[ctx], weight_send.at[0], weight_recv.at[0], across)
-    )
-    weight_all[ctx] = weight_ref[...]
+    meta_all[me] = meta_out[me]
     columns = pl.ds(pl.multiple_of(head * quarter, quarter), quarter)
-    cot_gather = Gather(
-        n_exp, cot_ref.at[:, columns], lambda index: cot_all.at[index], cot_send, cot_recv
-    )
-    cot_gather.start()
-    cot_all[me] = cot_ref[:, columns]
     for sem, device, _, from_block in others:
         remote(
             meta_all.at[from_block],
@@ -424,13 +435,30 @@
             meta_recv.at[sem],
             device,
         ).wait_recv()
-    kv_gather.finish()
-
     total = kv_all.shape[1]
     key_doc = jnp.concatenate([meta_all[s, 2:3, :] for s in range(total // rows)], axis=1)
     key_pos = lax.broadcasted_iota(jnp.int32, (rows, total), 1)
     query_pos = me * rows + lax.broadcasted_iota(jnp.int32, (rows, total), 0)
-    visible = (key_pos <= query_pos) & (key_doc == doc_ref[:, 0:1])
+    visible = (key_pos <= query_pos) & (key_doc == doc_column[:, 0:1])
+    kv_gather.forward()
+    begin(
+        remote(weight_ref, weight_all.at[ctx], weight_send.at[0], weight_recv.at[0], across)
+    )
+    weight_all[ctx] = weight_ref[...]
+    def place(e, s):
+        return pl.ds(pl.multiple_of((e * blocks + s) * capacity, 16), capacity)
+
+    for e in range(experts):
+        for s in range(blocks):
+            weight, rank = meta_all[s, e : e + 1, :], meta_all[s, 4 + e : 5 + e, :]
+            slot = lax.broadcasted_iota(jnp.int32, (capacity, rows), 0).astype(F32)
+            pick = jnp.where((slot == rank) & (weight > 0.0), 1.0, 0.0)
+            prob = jnp.sum(pick * weight, axis=1, keepdims=True)
+            picks[e * blocks + s] = pick.astype(BF16)
+            slot_prob[place(e, s), :] = jnp.broadcast_to(prob, (capacity, 128))
+
+    kv_gather.finish()
+
     scale = HEAD_DIMENSION ** (-0.5)
     heads = query_ref.shape[1] // HEAD_DIMENSION
     chunks = 4
@@ -485,34 +513,17 @@
         line_pass(c, 0)
         if c:
             line_pass(c - 1, 1)
-        if c == 2:
-            cot_gather.forward()
     line_pass(chunks - 1, 1)
     for c in range(chunks):
         line_pass(c, 2)
 
-    def place(e, s):
-        return pl.ds(pl.multiple_of((e * blocks + s) * capacity, 16), capacity)
-
-    cot_gather.finish()
-    for e in range(experts):
-
-        @pl.loop(0, blocks)
-        def _(s):
-            meta = meta_all[s]
-            weight, rank = meta[e : e + 1, :], meta[4 + e : 5 + e, :]
-            slot = lax.broadcasted_iota(jnp.int32, (capacity, rows), 0).astype(F32)
-            pick = jnp.where((slot == rank) & (weight > 0.0), 1.0, 0.0)
-            prob = jnp.sum(pick * weight, axis=1, keepdims=True)
-            pick = pick.astype(BF16)
-            picks[e * blocks + s] = pick
-            slot_prob[place(e, s), :] = jnp.broadcast_to(prob, (capacity, 128))
-            slot_grad[place(e, s), :] = (
-                prob * jnp.dot(pick, cot_all[s], preferred_element_type=F32)
-            ).astype(BF16)
-
     for c in range(chunks):
         line_pass(c, 3)
+    cot_gather = Gather(
+        n_exp, cot_ref.at[:, columns], lambda index: cot_all.at[index], cot_send, cot_recv
+    )
+    cot_gather.start()
+    cot_all[me] = cot_ref[:, columns]
     weight_view = weight_all.at[1 - ctx]
     remote(
         weight_view, weight_view, weight_send.at[0], weight_recv.at[0], across
@@ -582,7 +593,8 @@
     layer_ref[...] = state
     state = state.astype(F32)
     squares = jnp.sum(state * state, axis=1, keepdims=True)
-    square_out[...] = jnp.broadcast_to(squares, square_out.shape)
+    squares = jnp.broadcast_to(squares, (rows, 128)).T[0:8, :]
+    square_out[...] = squares
     square_copies = []
     for r in (2, 3, 1):
         copy = remote(
@@ -594,11 +606,13 @@
         )
         begin(copy)
         square_copies.append(copy)
+    cot_gather.forward()
     for copy in square_copies:
         copy.wait_recv()
     for r in range(3):
-        squares = squares + square_in[r][:, 0:1]
+        squares = squares + square_in[r]
     inverse = lax.rsqrt(squares / width + 1e-06)
+    inverse = jnp.broadcast_to(inverse[0:1, :], (rows, 128)).T[:, 0:1]
     normed = (state * inverse * gain_ref[:, columns]).astype(BF16)
     own_normed[...] = normed
     token_gather = Gather(
@@ -670,15 +684,19 @@
         act_copy(kind, e, head ^ 1, 1).wait_recv()
         act_copy(kind, e, head ^ 3, 2).wait_recv()
 
-    reduce_start(2, 0)
-    token_gather.forward()
-    for e in range(1, experts):
+    cot_gather.finish()
+    for e in range(experts):
+        for s in range(blocks):
+            slot_grad[place(e, s), :] = (
+                slot_prob[place(e, s), 0:1]
+                * jnp.dot(picks[e * blocks + s], cot_all[s], preferred_element_type=F32)
+            ).astype(BF16)
         reduce_start(2, e)
+        if e == 0:
+            token_gather.forward()
     token_gather.finish()
     for e in range(experts):
-
-        @pl.loop(0, blocks)
-        def _(s):
+        for s in range(blocks):
             slot_in[place(e, s), :] = jnp.dot(
                 picks[e * blocks + s], normed_all[s], preferred_element_type=F32
             ).astype(BF16)
@@ -704,7 +722,6 @@
 
     for e in range(experts):
         pass_on(0, e)
-    for e in range(experts):
         grad = reduced(2, e)
         gate, up = own_sum[e], own_sum[experts + e]
         sigma = 1.0 / (1.0 + jnp.exp(-gate))
@@ -719,8 +736,7 @@
             out = out.astype(BF16).astype(F32)
             scaled[whole, :] = (slot_prob[whole, 0:1] * out).astype(BF16)
 
-    @pl.loop(0, blocks)
-    def _(s):
+    def combined(s):
         total = jnp.zeros((rows, quarter), F32)
         for e in range(experts):
             total = total + lax.dot_general(
@@ -729,31 +745,50 @@
                 (((0,), (0,)), ((), ())),
                 preferred_element_type=F32,
             )
-        back_out[s] = total.astype(BF16)
-
-    for sem, device, to_block, _ in others:
-        begin(
-            remote(
-                back_out.at[to_block],
-                back_in.at[sem],
-                back_send.at[sem],
-                back_recv.at[sem],
-                device,
-            )
-        )
-    for e in range(experts):
+        return total.astype(BF16)
+
+    turns = tuple(range(1, n_exp)) + (0,)
+    back_copies = {}
+    for dz in turns:
+        to_exp = lax.rem(exp + dz, n_exp)
+        back_out[dz] = combined((1 - ctx) * n_exp + to_exp)
+        back_copies[dz] = remote(
+            back_out.at[dz], back_in.at[dz], back_send.at[dz], back_recv.at[dz], across
+        )
+        begin(back_copies[dz])
+    weight_grad(0, 0, grad_down_ref, slot_grad)
+    total = layer_ref[...].astype(F32)
+    for dz in turns:
+        to_exp = lax.rem(exp + dz, n_exp)
+        near = combined(ctx * n_exp + to_exp).astype(F32)
+        back_copies[dz].wait_recv()
+        near = near + back_in[dz].astype(F32)
+        if dz == 0:
+            total = total + near
+            continue
+        n = n_exp + dz
+        back_out[n] = near.astype(BF16)
+        back_copies[n] = remote(
+            back_out.at[n],
+            back_in.at[n],
+            back_send.at[n],
+            back_recv.at[n],
+            ring_id(ctx, head, to_exp),
+        )
+        begin(back_copies[n])
+    own_back[...] = total
+    for e in range(1, experts):
         weight_grad(0, e, grad_down_ref, slot_grad)
     for e in range(experts):
         for kind, out in ((1, grad_gate_ref), (2, grad_up_ref)):
             pass_on(kind, e)
             spread_done(kind, e)
             weight_grad(kind, e, out, slot_in)
-    total = layer_ref[...].astype(F32) + back_out[me].astype(F32)
-    for sem, device, to_block, _ in others:
-        remote(
-            back_out.at[to_block], back_in.at[sem], back_send.at[sem], back_recv.at[sem], device
-        ).wait_recv()
-        total = total + back_in[sem].astype(F32)
+    total = own_back[...]
+    for dz in range(1, n_exp):
+        n = n_exp + dz
+        back_copies[n].wait_recv()
+        total = total + back_in[n].astype(F32)
     layer_ref[...] = total.astype(BF16)
     for copy in sent + kv_gather.sent + cot_gather.sent + token_gather.sent:
         copy.wait_send()
@@ -799,6 +834,8 @@
         or n_exp != n_head
         or experts_here != 2
         or capacity % 16
+        or rows != 128
+        or experts > 128
         or capacity * experts_here < rows
         or rotated_key_value_pairs.shape[2] != HEAD_DIMENSION
     ):
@@ -820,23 +857,7 @@
     vmem = pl.BlockSpec(memory_space=pltpu.VMEM)
     shape = jax.ShapeDtypeStruct
 
-    named = routes[:, :, None] == jnp.arange(experts, dtype=jnp.int32)[None, None, :]
-    share = jnp.sum(jnp.where(named, probs[:, :, None], 0.0), axis=1)
-    mask = jnp.any(named, axis=1).astype(BF16)
-    earlier = jnp.tril(jnp.ones((rows, rows), BF16), -1)
-    rank = jnp.dot(earlier, mask, preferred_element_type=F32)
-    doc = doc_ids.astype(F32)
-    spare = jnp.zeros((owners, 2, rows), F32)
-    meta = jnp.concatenate(
-        [
-            share.T.reshape(owners, 2, rows),
-            jnp.broadcast_to(doc[None], (owners, 2, rows)),
-            rank.T.reshape(owners, 2, rows),
-            spare,
-        ],
-        axis=1,
-    )
-    doc_column = jnp.broadcast_to(doc.T, (rows, 128))
+    meta_shape = (owners, 8, rows)
     total = owners * rows
     lanes = queries.shape[1]
     slots = experts_here * owners * capacity
@@ -846,20 +867,21 @@
     return pl.pallas_call(
         functools.partial(layer_kernel, n_exp, capacity),
         out_shape=(shape((rows, quarter), BF16), grad_shape, grad_shape, grad_shape),
-        in_specs=[vmem] * 11,
+        in_specs=[vmem] * 12,
         out_specs=(vmem,) * 4,
         scratch_shapes=[
             pltpu.VMEM((2, total, HEAD_DIMENSION), BF16),
             pltpu.VMEM((owners, rows, quarter), BF16),
-            pltpu.VMEM(meta.shape, F32),
+            pltpu.VMEM(meta_shape, F32),
+            pltpu.VMEM(meta_shape, F32),
             pltpu.VMEM((2, lanes, quarter // 2), BF16),
             pltpu.VMEM((n_exp, rows, lanes), BF16),
             pltpu.VMEM((3, rows, quarter), BF16),
             pltpu.VMEM((3, rows, quarter), BF16),
             pltpu.VMEM((2, rows, quarter // 2), BF16),
             pltpu.VMEM((2, rows, quarter // 2), BF16),
-            pltpu.VMEM((rows, 128), F32),
-            pltpu.VMEM((3, rows, 128), F32),
+            pltpu.VMEM((8, rows), F32),
+            pltpu.VMEM((3, 8, rows), F32),
             pltpu.VMEM((rows, quarter), BF16),
             pltpu.VMEM((owners, rows, quarter), BF16),
             pltpu.VMEM((slots, quarter), BF16),
@@ -875,6 +897,7 @@
             pltpu.VMEM((slots, quarter), BF16),
             pltpu.VMEM((owners, rows, quarter), BF16),
             pltpu.VMEM((owners, rows, quarter), BF16),
+            pltpu.VMEM((rows, quarter), F32),
             dma((owners,)),
             dma((owners,)),
         ]
@@ -894,8 +917,9 @@
     )(
         rotated_key_value_pairs,
         queries,
-        doc_column,
-        meta,
+        doc_ids,
+        routes,
+        probs,
         cotangent,
         out_weight,
         resid,

time: 160 us -> 155 us (0.969)
  Pallas kernels: 147 us -> 142 us
  other arithmetic: 2.77 us -> 0 us
  local copies, waits for them, and re-layouts: 8.29 us -> 10.3 us
    pallas_call x1, Pallas kernels: 147 us -> 142 us  [per_device(): pl.pallas_call(functools.partial(layer_kernel, n_exp, capacity), out_shap...]
    unnamed x8 -> x10, local copies, waits for them, and re-layouts: 7.46 us -> 10.3 us
where the time goes in v3:
time: 155 us; the launch traced here: 153 us
  Pallas kernels  142 us (92%)
  local copies, waits for them, and re-layouts  10.3 us (7%)
    pallas_call x1, Pallas kernels, per_device(): pl.pallas_call(functools.partial(layer_kernel, n_exp, capacity), out_shap...  142 us
    unnamed x10, local copies, waits for them, and re-layouts  10.3 us

profile of v3, /device:TPU:9, one launch (start us, length us, event | category | flops | bytes accessed | tf_op | source)
XLA Modules:
  0.0 153.1 jit_solution(10971670974173721386)
XLA Ops:
  0.6 1.4 copy.16.route_ref
  2.0 1.4 copy.17.prob_ref
  3.5 142.2 %shard_map.147 = (bf16[128,512]{1,0:T(8,128)(2,1)}, bf16[2,768,512]{2,1,0:T(8,128)(2,1)}, bf16[2,768,512]{2,1,0:T(8,128)(2,1)}, bf16[2,768,512]{2,1,0:T(8,128)(2,1)}) custom-call(bf16[2,128,128]{2,1,0:T(8,128)(2,1)} %kv_ref.1, bf16[128,1024]{1,0:T(8,128)(2,1)} %query_ref.1, s32[1,128]{1,0:T(1,128)} %doc_ref.1, s32[128,8]{1,0:T(8,128)} %copy.16.route_ref, ...), custom_call_target="tpu_custom_call" | custom-call | tf_op jit(solution)/shard_map/pallas_call | solution.py:867
  145.7 1.6 %copy.22 = bf16[128,512]{1,0:T(8,128)(2,1)} copy(bf16[128,512]{1,0:T(8,128)(2,1)} %get-tuple-element.8) | data formatting | bytes 262144
  147.2 0.0 copy-start.1
  147.2 2.8 %copy.23 = bf16[2,768,512]{2,1,0:T(8,128)(2,1)} copy(bf16[2,768,512]{2,1,0:T(8,128)(2,1)} %get-tuple-element.9) | data formatting | bytes 3145728
  150.0 0.0 copy-done.1
  150.0 0.0 copy-start
  150.0 1.1 copy.24
  151.1 0.8 copy-done
  152.0 1.1 copy.25
Async XLA Ops:
  147.2 2.8 %copy-start.1 = (bf16[2,768,512]{2,1,0:T(8,128)(2,1)S(1)}, bf16[2,768,512]{2,1,0:T(8,128)(2,1)}, u32[]{:S(2)}) copy-start(bf16[2,768,512]{2,1,0:T(8,128)(2,1)} %get-tuple-element.10) | copy-start | bytes 4718596
  150.0 2.0 %copy-start = (bf16[2,768,512]{2,1,0:T(8,128)(2,1)S(1)}, bf16[2,768,512]{2,1,0:T(8,128)(2,1)}, u32[]{:S(2)}) copy-start(bf16[2,768,512]{2,1,0:T(8,128)(2,1)} %get-tuple-element.11) | copy-start | bytes 4718596

commit v4 on v3

--- a/solution.py
+++ b/solution.py
@@ -308,13 +308,21 @@
     weight_ref,
     resid_ref,
     gain_ref,
+    gate_source,
+    up_source,
+    down_source,
+    layer_ref,
+    grad_gate_out,
+    grad_up_out,
+    grad_down_out,
     gate_ref,
     up_ref,
     down_ref,
-    layer_ref,
     grad_gate_ref,
     grad_up_ref,
     grad_down_ref,
+    whole,
+    projections,
     kv_all,
     cot_all,
     meta_out,
@@ -369,6 +377,8 @@
     act_recv,
     back_send,
     back_recv,
+    load_sem,
+    store_sem,
 ):
     ctx, head, exp = lax.axis_index("ctx"), lax.axis_index("head"), lax.axis_index("exp")
     me = ctx * n_exp + exp
@@ -379,17 +389,29 @@
     half = quarter // 2
     core_peer, side_peer = ring_id(ctx, head ^ 1, exp), ring_id(ctx, head ^ 2, exp)
     across = ring_id(1 - ctx, head, exp)
+    loads = [
+        pltpu.make_async_copy(source, target, load_sem.at[n])
+        for n, (source, target) in enumerate(
+            ((down_source, down_ref), (gate_source, gate_ref), (up_source, up_ref))
+        )
+    ]
+    for load in loads:
+        load.start()
     others = token_group(n_exp)
-    lane = lax.broadcasted_iota(jnp.int32, (rows, 128), 1)
-    weight_of = jnp.zeros((rows, 128), F32)
-    for k in range(route_ref.shape[1]):
+    named = lax.broadcasted_iota(jnp.int32, (experts * blocks, rows), 0)
+    weight_of = jnp.zeros(named.shape, F32)
+    for k in range(route_ref.shape[0]):
         weight_of = weight_of + jnp.where(
-            route_ref[:, k : k + 1] == lane, prob_ref[:, k : k + 1], 0.0
-        )
-    earlier = jnp.where(lax.broadcasted_iota(jnp.int32, (rows, 128), 0) > lane, 1.0, 0.0)
+            route_ref[k : k + 1, :] == named, prob_ref[k : k + 1, :], 0.0
+        )
+    square = (rows, rows)
+    earlier = lax.broadcasted_iota(jnp.int32, square, 0) < lax.broadcasted_iota(
+        jnp.int32, square, 1
+    )
     mask = jnp.where(weight_of > 0.0, 1.0, 0.0)
-    rank_of = jnp.dot(earlier.astype(BF16), mask.astype(BF16), preferred_element_type=F32)
-    weight_of, rank_of = weight_of.T, rank_of.T
+    rank_of = jnp.dot(
+        mask.astype(BF16), jnp.where(earlier, 1.0, 0.0).astype(BF16), preferred_element_type=F32
+    )
     doc_row = doc_ref[...].astype(F32)
     doc_column = jnp.broadcast_to(doc_row, (rows, 128)).T
     for owner in range(blocks):
@@ -529,15 +551,15 @@
         weight_view, weight_view, weight_send.at[0], weight_recv.at[0], across
     ).wait_recv()
 
-    def projected(index):
-        block = attn_all[index]
-        return jnp.concatenate(
-            [jnp.dot(block, weight_all[p], preferred_element_type=F32) for p in range(2)], axis=1
-        )
+    lines = attn_all[...].reshape(n_exp * rows, attn_all.shape[2])
+    for p in range(2):
+        projections[:, :, p * half : (p + 1) * half] = jnp.dot(
+            lines, weight_all[p], preferred_element_type=F32
+        ).reshape(n_exp, rows, half)
 
     part_copies = []
     for r in (2, 3, 1):
-        part_out[r - 1] = projected(head ^ r).astype(BF16)
+        part_out[r - 1] = projections[head ^ r].astype(BF16)
         copy = remote(
             part_out.at[r - 1],
             part_in.at[r - 1],
@@ -547,7 +569,7 @@
         )
         begin(copy)
         part_copies.append(copy)
-    state = projected(head)
+    state = projections[head]
     for copy in part_copies:
         copy.wait_recv()
     for r in range(3):
@@ -622,20 +644,11 @@
     normed_all[me] = normed
 
     kinds = ((slot_in, gate_ref), (slot_in, up_ref), (slot_grad, down_ref))
-    def rows_of(e, index):
-        return pl.ds(pl.multiple_of(e * 4 * share + index * share, 16), share)
-
     def own_rows(index):
         return pl.ds(pl.multiple_of(index * share, 16), share)
 
-    def partial(kind, e, index):
-        data, weight = kinds[kind]
-        return lax.dot_general(
-            data[rows_of(e, index), :],
-            weight[e],
-            (((1,), (1,)), ((), ())),
-            preferred_element_type=F32,
-        )
+    def partial(index):
+        return whole[own_rows(index), :]
 
     def core_copy(kind, e):
         n = kind * experts + e
@@ -651,14 +664,21 @@
 
     def reduce_start(kind, e):
         n = kind * experts + e
-        core_out[n, 1] = partial(kind, e, head ^ 3).astype(BF16)
-        core_out[n, 0] = partial(kind, e, head ^ 1).astype(BF16)
+        data, weight = kinds[kind]
+        whole[...] = lax.dot_general(
+            data[pl.ds(e * 4 * share, 4 * share), :],
+            weight[e],
+            (((1,), (1,)), ((), ())),
+            preferred_element_type=F32,
+        )
+        core_out[n, 1] = partial(head ^ 3).astype(BF16)
+        core_out[n, 0] = partial(head ^ 1).astype(BF16)
         begin(core_copy(kind, e))
-        crossing = partial(kind, e, head ^ 2)
+        crossing = partial(head ^ 2)
         core_copy(kind, e).wait_recv()
         side_out[n] = (crossing + core_in[n, 1].astype(F32)).astype(BF16)
         begin(side_copy(kind, e))
-        own_sum[n] = partial(kind, e, head) + core_in[n, 0].astype(F32)
+        own_sum[n] = partial(head) + core_in[n, 0].astype(F32)
 
     def reduced(kind, e):
         n = kind * experts + e
@@ -685,6 +705,8 @@
         act_copy(kind, e, head ^ 3, 2).wait_recv()
 
     cot_gather.finish()
+    for load in loads:
+        load.wait()
     for e in range(experts):
         for s in range(blocks):
             slot_grad[place(e, s), :] = (
@@ -709,6 +731,9 @@
         sigma = 1.0 / (1.0 + jnp.exp(-gate))
         spread(0, e, (gate * sigma * up).astype(BF16))
 
+    results = ((grad_down_out, 0), (grad_gate_out, 1), (grad_up_out, 2))
+    stores = []
+
     def weight_grad(kind, e, out, data):
         n = kind * experts + e
         source = data[pl.ds(e * 4 * share, 4 * share), :]
@@ -719,6 +744,12 @@
                 (((0,), (0,)), ((), ())),
                 preferred_element_type=F32,
             ).astype(BF16)
+        target, number = results[kind]
+        store = pltpu.make_async_copy(
+            out.at[e], target.at[e], store_sem.at[number * experts + e]
+        )
+        store.start()
+        stores.append(store)
 
     for e in range(experts):
         pass_on(0, e)
@@ -729,12 +760,10 @@
         spread(2, e, (grad * gate * sigma).astype(BF16))
     for e in range(experts):
         spread_done(0, e)
-        for index in range(4):
-            part = pl.ds(index * share, share)
-            whole = pl.ds((e * 4 + index) * share, share)
-            out = jnp.dot(acts[e, part, :], down_ref[e], preferred_element_type=F32)
-            out = out.astype(BF16).astype(F32)
-            scaled[whole, :] = (slot_prob[whole, 0:1] * out).astype(BF16)
+        place_all = pl.ds(e * 4 * share, 4 * share)
+        out = jnp.dot(acts[e], down_ref[e], preferred_element_type=F32)
+        out = out.astype(BF16).astype(F32)
+        scaled[place_all, :] = (slot_prob[place_all, 0:1] * out).astype(BF16)
 
     def combined(s):
         total = jnp.zeros((rows, quarter), F32)
@@ -790,6 +819,8 @@
         back_copies[n].wait_recv()
         total = total + back_in[n].astype(F32)
     layer_ref[...] = total.astype(BF16)
+    for store in stores:
+        store.wait()
     for copy in sent + kv_gather.sent + cot_gather.sent + token_gather.sent:
         copy.wait_send()
     for p in range(2):
@@ -855,6 +886,7 @@
         )
     dma = pltpu.SemaphoreType.DMA
     vmem = pl.BlockSpec(memory_space=pltpu.VMEM)
+    anywhere = pl.BlockSpec(memory_space=pl.ANY)
     shape = jax.ShapeDtypeStruct
 
     meta_shape = (owners, 8, rows)
@@ -867,9 +899,12 @@
     return pl.pallas_call(
         functools.partial(layer_kernel, n_exp, capacity),
         out_shape=(shape((rows, quarter), BF16), grad_shape, grad_shape, grad_shape),
-        in_specs=[vmem] * 12,
-        out_specs=(vmem,) * 4,
-        scratch_shapes=[
+        in_specs=[vmem] * 9 + [anywhere] * 3,
+        out_specs=(vmem,) + (anywhere,) * 3,
+        scratch_shapes=[pltpu.VMEM(w_gate.shape, BF16)] * 6
+        + [
+            pltpu.VMEM((4 * quarter_rows, hidden_units), F32),
+            pltpu.VMEM((n_exp, rows, quarter), F32),
             pltpu.VMEM((2, total, HEAD_DIMENSION), BF16),
             pltpu.VMEM((owners, rows, quarter), BF16),
             pltpu.VMEM(meta_shape, F32),
@@ -910,7 +945,8 @@
         + [dma((2 * n_exp,))] * 2
         + [dma((pairs,))] * 4
         + [dma((3 * pairs,))] * 2
-        + [dma((owners,))] * 2,
+        + [dma((owners,))] * 2
+        + [dma((3,)), dma((pairs,))],
         compiler_params=pltpu.CompilerParams(
             collective_id=1, has_side_effects=True, vmem_limit_bytes=58 << 20
         ),
@@ -918,8 +954,8 @@
         rotated_key_value_pairs,
         queries,
         doc_ids,
-        routes,
-        probs,
+        routes.T,
+        probs.T,
         cotangent,
         out_weight,
         resid,

time: 155 us -> 150 us (0.968)
  local copies, waits for them, and re-layouts: 10.3 us -> 7.46 us
  Pallas kernels: 142 us -> 140 us
    unnamed x10 -> x8, local copies, waits for them, and re-layouts: 10.3 us -> 7.46 us
    pallas_call x1, Pallas kernels: 142 us -> 140 us  [per_device(): pl.pallas_call(functools.partial(layer_kernel, n_exp, capacity), out_shap...]
where the time goes in v4:
time: 150 us; the launch traced here: 148 us
  Pallas kernels  140 us (93%)
  local copies, waits for them, and re-layouts  7.46 us (5%)
    pallas_call x1, Pallas kernels, per_device(): pl.pallas_call(functools.partial(layer_kernel, n_exp, capacity), out_shap...  140 us
    unnamed x8, local copies, waits for them, and re-layouts  7.46 us

profile of v4, /device:TPU:9, one launch (start us, length us, event | category | flops | bytes accessed | tf_op | source)
XLA Modules:
  0.0 147.6 jit_solution(3107091943763809526)
XLA Ops:
  0.6 139.5 %shard_map.147 = (bf16[128,512]{1,0:T(8,128)(2,1)}, bf16[2,768,512]{2,1,0:T(8,128)(2,1)}, bf16[2,768,512]{2,1,0:T(8,128)(2,1)}, bf16[2,768,512]{2,1,0:T(8,128)(2,1)}) custom-call(bf16[2,128,128]{2,1,0:T(8,128)(2,1)} %kv_ref.1, bf16[128,1024]{1,0:T(8,128)(2,1)} %query_ref.1, s32[1,128]{1,0:T(1,128)} %doc_ref.1, s32[8,128]{1,0:T(8,128)} %bitcast.4, ...), custom_call_target="tpu_custom_call" | custom-call | tf_op jit(solution)/shard_map/pallas_call | solution.py:899
  140.2 1.6 %copy.20 = bf16[128,512]{1,0:T(8,128)(2,1)} copy(bf16[128,512]{1,0:T(8,128)(2,1)} %get-tuple-element.8) | data formatting | bytes 262144
  141.7 0.0 copy-start.1
  141.7 2.8 %copy.21 = bf16[2,768,512]{2,1,0:T(8,128)(2,1)} copy(bf16[2,768,512]{2,1,0:T(8,128)(2,1)} %get-tuple-element.9) | data formatting | bytes 3145728
  144.5 0.0 copy-done.1
  144.5 0.0 copy-start
  144.5 1.1 copy.22
  145.6 0.8 copy-done
  146.5 1.1 copy.23
Async XLA Ops:
  141.7 2.8 %copy-start.1 = (bf16[2,768,512]{2,1,0:T(8,128)(2,1)S(1)}, bf16[2,768,512]{2,1,0:T(8,128)(2,1)}, u32[]{:S(2)}) copy-start(bf16[2,768,512]{2,1,0:T(8,128)(2,1)} %get-tuple-element.10) | copy-start | bytes 4718596
  144.5 2.0 %copy-start = (bf16[2,768,512]{2,1,0:T(8,128)(2,1)S(1)}, bf16[2,768,512]{2,1,0:T(8,128)(2,1)}, u32[]{:S(2)}) copy-start(bf16[2,768,512]{2,1,0:T(8,128)(2,1)} %get-tuple-element.11) | copy-start | bytes 4718596

commit v5 on v4

--- a/solution.py
+++ b/solution.py
@@ -539,13 +539,13 @@
     for c in range(chunks):
         line_pass(c, 2)
 
+    cot_gather = Gather(
+        n_exp, cot_ref.at[:, columns], lambda index: cot_all.at[index], cot_send, cot_recv
+    )
+    cot_gather.start()
+    cot_all[me] = cot_ref[:, columns]
     for c in range(chunks):
         line_pass(c, 3)
-    cot_gather = Gather(
-        n_exp, cot_ref.at[:, columns], lambda index: cot_all.at[index], cot_send, cot_recv
-    )
-    cot_gather.start()
-    cot_all[me] = cot_ref[:, columns]
     weight_view = weight_all.at[1 - ctx]
     remote(
         weight_view, weight_view, weight_send.at[0], weight_recv.at[0], across

time: 150 us -> 151 us (level); the launches traced: 148 us -> 151 us
  Pallas kernels: 140 us -> 143 us
    pallas_call x1, Pallas kernels: 140 us -> 143 us  [per_device(): pl.pallas_call(functools.partial(layer_kernel, n_exp, capacity), out_shap...]
where the time goes in v5:
time: 151 us
  Pallas kernels  143 us (95%)
  local copies, waits for them, and re-layouts  7.46 us (5%)
    pallas_call x1, Pallas kernels, per_device(): pl.pallas_call(functools.partial(layer_kernel, n_exp, capacity), out_shap...  143 us
    unnamed x8, local copies, waits for them, and re-layouts  7.46 us

profile of v5, /device:TPU:9, one launch (start us, length us, event | category | flops | bytes accessed | tf_op | source)
XLA Modules:
  0.0 151.0 jit_solution(12106507088336675625)
XLA Ops:
  0.6 142.9 %shard_map.147 = (bf16[128,512]{1,0:T(8,128)(2,1)}, bf16[2,768,512]{2,1,0:T(8,128)(2,1)}, bf16[2,768,512]{2,1,0:T(8,128)(2,1)}, bf16[2,768,512]{2,1,0:T(8,128)(2,1)}) custom-call(bf16[2,128,128]{2,1,0:T(8,128)(2,1)} %kv_ref.1, bf16[128,1024]{1,0:T(8,128)(2,1)} %query_ref.1, s32[1,128]{1,0:T(1,128)} %doc_ref.1, s32[8,128]{1,0:T(8,128)} %bitcast.4, ...), custom_call_target="tpu_custom_call" | custom-call | tf_op jit(solution)/shard_map/pallas_call | solution.py:899
  143.5 1.6 %copy.20 = bf16[128,512]{1,0:T(8,128)(2,1)} copy(bf16[128,512]{1,0:T(8,128)(2,1)} %get-tuple-element.8) | data formatting | bytes 262144
  145.1 0.0 copy-start.1
  145.1 2.8 %copy.21 = bf16[2,768,512]{2,1,0:T(8,128)(2,1)} copy(bf16[2,768,512]{2,1,0:T(8,128)(2,1)} %get-tuple-element.9) | data formatting | bytes 3145728
  147.8 0.0 copy-done.1
  147.9 0.0 copy-start
  147.9 1.1 copy.22
  149.0 0.8 copy-done
  149.8 1.1 copy.23
Async XLA Ops:
  145.1 2.8 %copy-start.1 = (bf16[2,768,512]{2,1,0:T(8,128)(2,1)S(1)}, bf16[2,768,512]{2,1,0:T(8,128)(2,1)}, u32[]{:S(2)}) copy-start(bf16[2,768,512]{2,1,0:T(8,128)(2,1)} %get-tuple-element.10) | copy-start | bytes 4718596
  147.9 2.0 %copy-start = (bf16[2,768,512]{2,1,0:T(8,128)(2,1)S(1)}, bf16[2,768,512]{2,1,0:T(8,128)(2,1)}, u32[]{:S(2)}) copy-start(bf16[2,768,512]{2,1,0:T(8,128)(2,1)} %get-tuple-element.11) | copy-start | bytes 4718596
